TPU v7x, 32 devices: a whole 2x2x4 slice. The times are simulated.
32 devices in a mesh: ctx: 16 (over z, x, core), head: 2 (over y).
Axes of the slice: x: 2, y: 2, z: 4, core: 2. Of those that a mesh axis runs over, the one named last changes fastest.
Arguments:
- queries: bfloat16 [8192, 8192], P('ctx', 'head'), may hold values from -128 to 128
- key_rows: bfloat16 [8192, 1024], P(('ctx', 'head')), may hold values from -8 to 8
- value_rows: bfloat16 [8192, 1024], P(('ctx', 'head')), may hold values from -6 to 6
- grad_output: bfloat16 [8192, 8192], P('ctx', 'head'), may hold values from -6 to 6
- doc_lengths: int32 [32], replicated, may hold values from 1 to 512, 8192 in all
Outputs:
- grad_queries: bfloat16 [8192, 8192], P('ctx', 'head')
- grad_keys: bfloat16 [8192, 1024], P(('ctx', 'head'))
- grad_values: bfloat16 [8192, 1024], P(('ctx', 'head'))
Inputs may be any that keep to these rules, and one draw needn't show every extreme that they name: `doc_lengths`: document lengths sum to 8192; the longest is exactly 512.
All inputs are finite; a program needn't handle non-finite values.
Results may differ from a plain program's by a relative error of at most 0.02.
Values may be sent and summed in bfloat16 or wider, within the bound.
No kernel may reach another device: no remote copies, remote signals or barrier semaphores. Data moves between devices by JAX's collectives and lax.ppermute only.
A program may use at most 256 MiB of HBM per device.

v0:
```python
import math

import jax
import jax.numpy as jnp
from jax import lax
from jax.sharding import PartitionSpec as P

H = 64
KVH = 8
HD = 128


def shifted(value, axis, steps):
    count = lax.axis_size(axis)
    initial, last = (max(0, -steps), min(count, count - steps))
    return lax.ppermute(value, axis, [(source, source + steps) for source in range(initial, last)])


def segment_of(places, bounds):
    return jnp.sum((places[:, None] >= bounds[None, :]).astype(jnp.int32), axis=1)


def scores(query_loc, key_part, allowed, factor):
    logits = (
        jnp.einsum("rkgd,wkd->kgrw", query_loc, key_part, preferred_element_type=jnp.float32)
        * factor
    )
    return jnp.where(allowed[None, None], logits, -1e30)


def normalize(logit_list, value_list, grad_loc):
    maximum = logit_list[0].max(axis=-1, keepdims=True)
    raised = [jnp.exp(logits - maximum) for logits in logit_list]
    denominator = raised[0].sum(axis=-1, keepdims=True)
    weights = [value / denominator for value in raised]
    weights_low = [value.astype(jnp.bfloat16) for value in weights]
    output = jnp.einsum(
        "kgrw,wkd->rkgd", weights_low[0], value_list[0], preferred_element_type=jnp.float32
    )
    output = output.astype(jnp.bfloat16)
    deltas = jnp.transpose(
        jnp.sum(grad_loc.astype(jnp.float32) * output.astype(jnp.float32), axis=-1), (1, 2, 0)
    )[..., None]
    return (weights, weights_low, deltas)


def backward_part(weights, weights_low, grad_loc, value_part, key_part, query_loc, deltas, factor):
    grad_weights = jnp.einsum(
        "rkgd,wkd->kgrw", grad_loc, value_part, preferred_element_type=jnp.float32
    )
    grad_logits = (weights * (grad_weights - deltas)).astype(jnp.bfloat16)
    grad_query = jnp.einsum(
        "kgrw,wkd->rkgd", grad_logits, key_part, preferred_element_type=jnp.float32
    )
    grad_key = (
        jnp.einsum("kgrw,rkgd->wkd", grad_logits, query_loc, preferred_element_type=jnp.float32)
        * factor
    )
    grad_val = jnp.einsum(
        "kgrw,rkgd->wkd", weights_low, grad_loc, preferred_element_type=jnp.float32
    )
    return (grad_query, grad_key, grad_val)


def fetch_window(key_rows, value_rows):
    key_own, val_own = (
        lax.all_to_all(key_rows, "head", split_axis=1, concat_axis=0, tiled=True),
        lax.all_to_all(value_rows, "head", split_axis=1, concat_axis=0, tiled=True),
    )
    arrived = shifted(jnp.stack([key_own, val_own]), "ctx", 1)
    return (key_own, val_own, arrived[0], arrived[1])


def return_prev(key_own_grad, val_own_grad, key_prev_grad, val_prev_grad, row_count):
    arrived = shifted(jnp.stack([key_prev_grad, val_prev_grad]), "ctx", -1)
    key_total = (key_own_grad + arrived[0]).reshape(row_count, -1).astype(jnp.bfloat16)
    val_total = (val_own_grad + arrived[1]).reshape(row_count, -1).astype(jnp.bfloat16)
    grad_keys, grad_values = (
        lax.all_to_all(key_total, "head", split_axis=0, concat_axis=1, tiled=True),
        lax.all_to_all(val_total, "head", split_axis=0, concat_axis=1, tiled=True),
    )
    return (grad_keys, grad_values)


def per_device(queries, key_rows, value_rows, grad_output, doc_lengths):
    row_count = queries.shape[0]
    kv_local = KVH // lax.axis_size("head")
    groups = H // KVH
    factor = 1.0 / math.sqrt(HD)
    shard_index = lax.axis_index("ctx")
    bounds = jnp.cumsum(doc_lengths)
    own_pos = shard_index * row_count + jnp.arange(row_count, dtype=jnp.int32)
    own_seg = segment_of(own_pos, bounds)
    prev_pos = own_pos - row_count
    prev_seg = jnp.where(prev_pos >= 0, segment_of(prev_pos, bounds), -1)
    own_mask = (own_seg[:, None] == own_seg[None, :]) & (own_pos[None, :] <= own_pos[:, None])
    prev_mask = own_seg[:, None] == prev_seg[None, :]
    key_own, val_own, key_prev, val_prev = fetch_window(key_rows, value_rows)
    key_own = key_own.reshape(row_count, kv_local, HD)
    val_own = val_own.reshape(row_count, kv_local, HD)
    key_prev = key_prev.reshape(row_count, kv_local, HD)
    val_prev = val_prev.reshape(row_count, kv_local, HD)
    query_loc = queries.reshape(row_count, kv_local, groups, HD)
    grad_loc = grad_output.reshape(row_count, kv_local, groups, HD)
    key_win = jnp.concatenate([key_prev, key_own], axis=0)
    val_win = jnp.concatenate([val_prev, val_own], axis=0)
    allowed = jnp.concatenate([prev_mask, own_mask], axis=1)
    logits = scores(query_loc, key_win, allowed, factor)
    weights, weights_low, deltas = normalize([logits], [val_win], grad_loc)
    grad_query, grad_key, grad_val = backward_part(
        weights[0], weights_low[0], grad_loc, val_win, key_win, query_loc, deltas, factor
    )
    grad_keys, grad_values = return_prev(
        grad_key[row_count:],
        grad_val[row_count:],
        grad_key[:row_count],
        grad_val[:row_count],
        row_count,
    )
    grad_queries = (grad_query * factor).reshape(row_count, -1).astype(jnp.bfloat16)
    return (grad_queries, grad_keys, grad_values)


def solution(mesh):
    in_specs = (
        P("ctx", "head"),
        P(("ctx", "head"), None),
        P(("ctx", "head"), None),
        P("ctx", "head"),
        P(),
    )
    out_specs = (P("ctx", "head"), P(("ctx", "head"), None), P(("ctx", "head"), None))
    return jax.shard_map(
        per_device, mesh=mesh, in_specs=in_specs, out_specs=out_specs, check_vma=False
    )
```

profile of v0, /device:TPU:15, one launch (start us, length us, event | category | flops | bytes accessed | tf_op | source)
XLA Modules:
  0.0 264.1 jit_solution(10178360844085025115)
XLA Ops:
  0.6 0.0 copy-start.1
  0.6 2.0 copy.67
  2.7 3.7 %all-to-all-start = ((bf16[256,2,512]{0,2,1:T(8,128)(2,1)}), bf16[256,2,512]{0,2,1:T(8,128)(2,1)S(1)}, u32[]{:S(2)}, u32[]{:S(2)}) async-start(bf16[256,2,512]{0,2,1:T(8,128)(2,1)} %bitcast), calls=%async_computation | async-start | bytes 1048576 | tf_op jit(solution)/shard_map/all_to_all | solution.py:67
  6.4 2.0 copy.69
  8.4 4.2 %all-to-all-done = bf16[256,2,512]{0,2,1:T(8,128)(2,1)S(1)} async-done(((bf16[256,2,512]{0,2,1:T(8,128)(2,1)}), bf16[256,2,512]{0,2,1:T(8,128)(2,1)S(1)}, u32[]{:S(2)}, u32[]{:S(2)}) %all-to-all-start) | async-done | bytes 524320 | tf_op jit(solution)/shard_map/all_to_all | solution.py:67
  12.6 4.6 %all-to-all-start.1 = ((bf16[256,2,512]{0,2,1:T(8,128)(2,1)}), bf16[256,2,512]{0,2,1:T(8,128)(2,1)S(1)}, u32[]{:S(2)}, u32[]{:S(2)}) async-start(bf16[256,2,512]{0,2,1:T(8,128)(2,1)} %bitcast.3), calls=%async_computation.1 | async-start | bytes 1048576 | tf_op jit(solution)/shard_map/all_to_all | solution.py:68
  17.3 0.2 copy.68
  17.5 5.1 %all-to-all-done.1 = bf16[256,2,512]{0,2,1:T(8,128)(2,1)S(1)} async-done(((bf16[256,2,512]{0,2,1:T(8,128)(2,1)}), bf16[256,2,512]{0,2,1:T(8,128)(2,1)S(1)}, u32[]{:S(2)}, u32[]{:S(2)}) %all-to-all-start.1) | async-done | bytes 524320 | tf_op jit(solution)/shard_map/all_to_all | solution.py:68
  22.5 0.2 copy.70
  22.8 0.1 pad_maximum_fusion.1
  22.9 5.3 %collective-permute-start = (bf16[2,512,512]{2,1,0:T(8,128)(2,1)S(1)}, bf16[2,512,512]{2,1,0:T(8,128)(2,1)}, u32[]{:S(2)}, u32[]{:S(2)}) collective-permute-start(bf16[2,512,512]{2,1,0:T(8,128)(2,1)S(1)} %pad_maximum_fusion.1), channel_id=1, source_target_pairs={{0,2},{2,4},{4,6},{6,8},{8,10},{10,12},{12,14},{14,16},{16,18},{18... | collective-permute-start | bytes 3145736 | tf_op jit(solution)/shard_map/ppermute | solution.py:16
  28.1 0.0 copy-done.1
  28.1 0.1 copy.75
  28.2 0.1 reduce-window.8
  28.3 0.1 reduce
  28.4 5.4 %copy.110 = bf16[64,8,32,128]{3,2,1,0:T(8,128)(2,1)} copy(bf16[64,8,32,128]{3,1,2,0:T(8,128)(2,1)} %bitcast.111) | data formatting | bytes 8388608
  33.8 6.4 %copy.81 = bf16[512,4096]{0,1:T(8,128)(2,1)} copy(bf16[512,4096]{1,0:T(8,128)(2,1)} %param.8) | data formatting | bytes 8388608 | tf_op args[3]
  40.2 0.1 convert_reduce_fusion
  40.3 0.4 broadcast_compare_fusion
  40.8 0.8 pad_add_fusion
  41.6 0.1 reshape.90
  41.7 0.1 reshape.94
  41.8 0.1 copy.74
  41.9 0.1 copy.80
  42.0 0.0 collective-permute-done
  42.0 1.3 fusion.36
  43.3 0.2 copy.77
  43.5 0.3 copy.79
  43.8 0.2 copy.71
  44.0 0.3 copy.73
  44.3 29.5 %fusion.37 = (f32[4,8,512]{2,1,0:T(8,128)S(1)}, f32[4,8,512,1024]{2,3,1,0:T(8,128)}) fusion(pred[512,1024]{0,1:T(8,128)(4,1)} %pad_add_fusion, bf16[512,4,8,128]{3,2,1,0:T(8,128)(2,1)} %bitcast.112, bf16[512,4,128]{2,0,1:T(8,128)(2,1)S(1)} %copy.74, bf16[512,4,128]{2,0,1:T(8,128)(2,1)S(1)} %copy.73), kind=kOutput, calls=%fused_computation.52 | convolution fusion | flops 4364174336 | bytes 72941568 | tf_op jit(solution)/shard_map/sub | solution.py:33
  73.8 32.9 %fusion.7 = bf16[4,8,512,1024]{2,3,1,0:T(8,128)(2,1)} fusion(f32[4,8,512,1024]{2,3,1,0:T(8,128)} %get-tuple-element.24, f32[4,8,512]{2,1,0:T(8,128)S(1)} %get-tuple-element.23), kind=kLoop, calls=%fused_computation.11 | loop fusion | flops 33554432 | bytes 100728832 | tf_op jit(solution)/shard_map/convert_element_type | solution.py:36
  106.7 17.2 %convolution_bitcast_fusion = f32[1024,4,128]{2,0,1:T(8,128)} fusion(bf16[4,8,512,1024]{2,3,1,0:T(8,128)(2,1)} %fusion.7, bf16[512,4,8,128]{0,3,2,1:T(8,128)(2,1)} %bitcast.105), kind=kOutput, calls=%fused_computation.25 | convolution fusion | flops 4294967296 | bytes 39845888 | tf_op jit(solution)/shard_map/kgrw,rkgd->wkd/dot_general | solution.py:59
  123.9 16.4 %fusion.10 = f32[512,4,8]{0,2,1:T(8,128)S(1)} fusion(bf16[512,4,8,128]{0,3,2,1:T(8,128)(2,1)} %bitcast.106, bf16[4,8,512,1024]{2,3,1,0:T(8,128)(2,1)} %fusion.7, bf16[512,4,128]{2,0,1:T(8,128)(2,1)S(1)} %copy.80, bf16[512,4,128]{2,0,1:T(8,128)(2,1)S(1)} %copy.79), kind=kOutput, calls=%fused_computation.14 | convolution fusion | flops 4307533824 | bytes 38862848 | tf_op jit(solution)/shard_map/kgrw,wkd->rkgd/dot_general | solution.py:37
  140.3 36.1 %fusion.2 = bf16[4,8,512,1024]{2,3,1,0:T(8,128)(2,1)} fusion(bf16[512,4,8,128]{0,3,2,1:T(8,128)(2,1)} %bitcast.107, f32[4,8,512]{2,1,0:T(8,128)S(1)} %bitcast.122, f32[4,8,512,1024]{2,3,1,0:T(8,128)} %get-tuple-element.24, f32[4,8,512]{2,1,0:T(8,128)S(1)} %get-tuple-element.23, bf16[512,4,128]{2,0,1:T(8,128)(2,1)S(1)} %copy.80, ...), kind=kOutput, calls=%fused_computation.3 | convolution fusion | flops 4364173312 | bytes 106037248 | tf_op jit(solution)/shard_map/rkgd,wkd->kgrw/dot_general | solution.py:48
  176.4 0.0 copy-start
  176.4 16.4 %fusion.20 = f32[1024,4,128]{2,0,1:T(8,128)S(1)} fusion(bf16[4,8,512,1024]{2,3,1,0:T(8,128)(2,1)} %fusion.2, bf16[512,4,8,128]{3,2,1,0:T(8,128)(2,1)} %bitcast.113), kind=kOutput, calls=%fused_computation.23 | convolution fusion | flops 4295491584 | bytes 39845888 | tf_op jit(solution)/shard_map/kgrw,rkgd->wkd/dot_general | solution.py:56
  192.9 0.1 slice_bitcast_fusion.3
  192.9 0.0 copy-done
  193.0 0.1 slice_bitcast_fusion.2
  193.0 0.1 pad_maximum_fusion
  193.2 2.1 collective-permute-start.1
  195.3 26.3 %collective-permute-done.1 = f32[2,512,4,128]{3,1,2,0:T(8,128)S(1)} collective-permute-done((f32[2,512,4,128]{3,1,2,0:T(8,128)S(1)}, f32[2,512,4,128]{3,1,2,0:T(8,128)S(1)}, u32[]{:S(2)}, u32[]{:S(2)}) %collective-permute-start.1) | collective-permute-done | bytes 2097184 | tf_op jit(solution)/shard_map/ppermute | solution.py:16
  221.6 0.2 fusion.24
  221.9 0.4 copy.91
  222.3 1.0 convert_element_type.62
  223.3 4.9 %all-to-all-start.3 = ((bf16[2,256,512]{2,1,0:T(8,128)(2,1)}), bf16[2,256,512]{2,1,0:T(8,128)(2,1)S(1)}, u32[]{:S(2)}, u32[]{:S(2)}) async-start(bf16[2,256,512]{2,1,0:T(8,128)(2,1)} %convert_element_type.62), calls=%async_computation.3 | async-start | bytes 1048576 | tf_op jit(solution)/shard_map/all_to_all | solution.py:80
  228.2 0.4 copy.89
  228.6 1.0 convert_element_type.60
  229.6 3.4 %all-to-all-done.3 = bf16[2,256,512]{2,1,0:T(8,128)(2,1)S(1)} async-done(((bf16[2,256,512]{2,1,0:T(8,128)(2,1)}), bf16[2,256,512]{2,1,0:T(8,128)(2,1)S(1)}, u32[]{:S(2)}, u32[]{:S(2)}) %all-to-all-start.3) | async-done | bytes 524320 | tf_op jit(solution)/shard_map/all_to_all | solution.py:80
  232.9 5.2 %all-to-all-start.2 = ((bf16[2,256,512]{2,1,0:T(8,128)(2,1)}), bf16[2,256,512]{2,1,0:T(8,128)(2,1)S(1)}, u32[]{:S(2)}, u32[]{:S(2)}) async-start(bf16[2,256,512]{2,1,0:T(8,128)(2,1)} %convert_element_type.60), calls=%async_computation.2 | async-start | bytes 1048576 | tf_op jit(solution)/shard_map/all_to_all | solution.py:79
  238.2 17.2 %multiply_convert_fusion = bf16[4,128,8,512]{3,1,2,0:T(8,128)(2,1)} fusion(bf16[4,8,512,1024]{2,3,1,0:T(8,128)(2,1)} %fusion.2, bf16[512,4,128]{2,0,1:T(8,128)(2,1)S(1)} %copy.74, bf16[512,4,128]{2,0,1:T(8,128)(2,1)S(1)} %copy.73), kind=kOutput, calls=%fused_computation.15 | convolution fusion | flops 4301258752 | bytes 38797312 | tf_op jit(solution)/shard_map/kgrw,wkd->rkgd/dot_general | solution.py:52
  255.3 6.3 %copy.93 = bf16[512,4096]{1,0:T(8,128)(2,1)} copy(bf16[512,4096]{0,1:T(8,128)(2,1)} %bitcast.108) | data formatting | bytes 8388608
  261.6 0.2 copy.92
  261.8 1.0 copy.95
  262.8 0.0 all-to-all-done.2
  262.8 0.2 copy.90
  263.1 1.0 copy.94
  (2 shorter events, 0.0 us)
Async XLA Ops:
  0.6 27.5 %copy-start.1 = (s32[32]{0:T(128)S(1)}, s32[32]{0:T(128)}, u32[]{:S(2)}) copy-start(s32[32]{0:T(128)} %param.9) | copy-start | bytes 388
  2.7 10.0 %all-to-all-start = ((bf16[256,2,512]{0,2,1:T(8,128)(2,1)}), bf16[256,2,512]{0,2,1:T(8,128)(2,1)S(1)}, u32[]{:S(2)}, u32[]{:S(2)}) async-start(bf16[256,2,512]{0,2,1:T(8,128)(2,1)} %bitcast), calls=%async_computation | async-start | bytes 1048576 | tf_op jit(solution)/shard_map/all_to_all | solution.py:67
  12.6 9.9 %all-to-all-start.1 = ((bf16[256,2,512]{0,2,1:T(8,128)(2,1)}), bf16[256,2,512]{0,2,1:T(8,128)(2,1)S(1)}, u32[]{:S(2)}, u32[]{:S(2)}) async-start(bf16[256,2,512]{0,2,1:T(8,128)(2,1)} %bitcast.3), calls=%async_computation.1 | async-start | bytes 1048576 | tf_op jit(solution)/shard_map/all_to_all | solution.py:68
  22.9 19.1 %collective-permute-start = (bf16[2,512,512]{2,1,0:T(8,128)(2,1)S(1)}, bf16[2,512,512]{2,1,0:T(8,128)(2,1)}, u32[]{:S(2)}, u32[]{:S(2)}) collective-permute-start(bf16[2,512,512]{2,1,0:T(8,128)(2,1)S(1)} %pad_maximum_fusion.1), channel_id=1, source_target_pairs={{0,2},{2,4},{4,6},{6,8},{8,10},{10,12},{12,14},{14,16},{16,18},{18... | collective-permute-start | bytes 3145736 | tf_op jit(solution)/shard_map/ppermute | solution.py:16
  176.4 16.5 %copy-start = (f32[1024,4,128]{2,0,1:T(8,128)S(1)}, f32[1024,4,128]{2,0,1:T(8,128)}, u32[]{:S(2)}) copy-start(f32[1024,4,128]{2,0,1:T(8,128)} %convolution_bitcast_fusion) | copy-start | bytes 6291460
  193.2 28.5 %collective-permute-start.1 = (f32[2,512,4,128]{3,1,2,0:T(8,128)S(1)}, f32[2,512,4,128]{3,1,2,0:T(8,128)S(1)}, u32[]{:S(2)}, u32[]{:S(2)}) collective-permute-start(f32[2,512,4,128]{3,1,2,0:T(8,128)S(1)} %pad_maximum_fusion), channel_id=1, source_target_pairs={{2,0},{4,2},{6,4},{8,6},{10,8},{12,10},{14,12},{16,14},{18,16},{20... | collective-permute-start | bytes 6291464 | tf_op jit(solution)/shard_map/ppermute | solution.py:16
  223.3 9.7 %all-to-all-start.3 = ((bf16[2,256,512]{2,1,0:T(8,128)(2,1)}), bf16[2,256,512]{2,1,0:T(8,128)(2,1)S(1)}, u32[]{:S(2)}, u32[]{:S(2)}) async-start(bf16[2,256,512]{2,1,0:T(8,128)(2,1)} %convert_element_type.62), calls=%async_computation.3 | async-start | bytes 1048576 | tf_op jit(solution)/shard_map/all_to_all | solution.py:80
  232.9 29.9 %all-to-all-start.2 = ((bf16[2,256,512]{2,1,0:T(8,128)(2,1)}), bf16[2,256,512]{2,1,0:T(8,128)(2,1)S(1)}, u32[]{:S(2)}, u32[]{:S(2)}) async-start(bf16[2,256,512]{2,1,0:T(8,128)(2,1)} %convert_element_type.60), calls=%async_computation.2 | async-start | bytes 1048576 | tf_op jit(solution)/shard_map/all_to_all | solution.py:79
where the time goes:
time: 266 us; the launch traced here: 264 us
  matrix products  133 us (50%)
  waiting for transfers between devices  39 us (15%)
  other arithmetic  34.8 us (13%)
  local copies, waits for them, and re-layouts  30.7 us (12%)
  starting transfers between devices  25.9 us (10%)
    dot_general x1, matrix products, backward_part(): jnp.einsum('rkgd,wkd->kgrw', grad_loc, value_part, preferred_element_type...  36.1 us
    convert_element_type x1, other arithmetic, normalize(): weights_low = [value.astype(jnp.bfloat16) for value in weights]  32.9 us
    sub x1, matrix products, normalize(): raised = [jnp.exp(logits - maximum) for logits in logit_list]  29.5 us
    ppermute x2, waiting for transfers between devices, shifted(): lax.ppermute(value, axis, [(source, source + steps) for source in range(i...  26.3 us
    unnamed x11, local copies, waits for them, and re-layouts  24.2 us
    dot_general x1, matrix products, backward_part(): jnp.einsum('kgrw,rkgd->wkd', weights_low, grad_loc, preferred_element_typ...  17.2 us
    dot_general x1, matrix products, backward_part(): jnp.einsum('kgrw,wkd->rkgd', grad_logits, key_part, preferred_element_typ...  17.2 us
    dot_general x1, matrix products, backward_part(): jnp.einsum('kgrw,rkgd->wkd', grad_logits, query_loc, preferred_element_ty...  16.4 us
  transfers between devices with their start and end apart: 6, of which 4 were waited for; matrix products, arithmetic and copies ran while one was open for 16% of the time, Pallas kernels for 0%

commit v1 on v0

v1 whole, which is shorter than its diff:
```python
import functools
import math

import jax
import jax.numpy as jnp
from jax import lax
from jax.experimental import pallas as pl
from jax.experimental.pallas import tpu as pltpu
from jax.sharding import PartitionSpec as P

H = 64
KVH = 8
HD = 128
G = H // KVH
NEG = -1e30
ROW_TILE = 128
HEADS_STEP = 2
BF16 = jnp.bfloat16
F32 = jnp.float32
NT = (((1,), (1,)), ((), ()))
NN = (((1,), (0,)), ((), ()))
TN = (((0,), (0,)), ((), ()))


def attn_kernel(info_ref, docs_ref, q_ref, do_ref, *refs, tokens, pieces, aliased):
    count = 2 * pieces
    k_in, v_in, refs = refs[:count], refs[count : 2 * count], refs[2 * count :]
    if aliased:
        refs = refs[1:]
    dq_ref, refs = refs[0], refs[1:]
    dk_out, dv_out, refs = refs[:count], refs[count : 2 * count], refs[2 * count :]
    k_win, v_win, dk_acc, dv_acc, bias, tiles = refs
    rt = ROW_TILE
    n_tiles = tokens // rt
    part = tokens // pieces
    scale = math.log2(math.e) / math.sqrt(HD)
    factor = 1.0 / math.sqrt(HD)
    base = info_ref[0] * tokens
    first_off = pl.multiple_of(info_ref[1], part)
    if pieces == 1:
        places = [0, tokens]
    else:
        second_off = pl.multiple_of(part - first_off, part)
        places = [first_off, second_off, tokens + first_off, tokens + second_off]

    @pl.when(pl.program_id(0) == 0)
    def _():
        pos = base + lax.broadcasted_iota(jnp.int32, (1, tokens), 1)

        def doc(i, carry):
            bound, start, firsts = carry
            bound = bound + docs_ref[i]
            start = jnp.where(pos >= bound, bound, start)
            firsts = tuple(
                jnp.where(base + r * rt >= bound, bound, f) for r, f in enumerate(firsts)
            )
            return bound, start, firsts

        zero = jnp.int32(0)
        _, start, firsts = lax.fori_loop(
            0, docs_ref.shape[0], doc, (zero, jnp.zeros((1, tokens), jnp.int32), (zero,) * n_tiles)
        )
        for r in range(n_tiles):
            tiles[r] = lax.div(base + (r + 1) * rt - 1 - firsts[r], rt) + 1
            key_pos = (
                base + r * rt - tokens + lax.broadcasted_iota(jnp.int32, (tokens + rt, rt), 0)
            )
            cols = slice(r * rt, (r + 1) * rt)
            ok = (key_pos >= start[:, cols]) & (key_pos <= pos[:, cols])
            bias[r] = jnp.where(ok, 0.0, NEG).astype(F32)

    for place, k, v in zip(places, k_in, v_in):
        k_win[pl.ds(place, part), :] = k[...]
        v_win[pl.ds(place, part), :] = v[...]
    dk_acc[...] = jnp.zeros_like(dk_acc)
    dv_acc[...] = jnp.zeros_like(dv_acc)

    def row_tile(r, _):
        row0 = pl.multiple_of(r * rt, rt)
        for n in range(1, n_tiles + 2):

            @pl.when(tiles[r] == n)
            def _(n=n):
                span = n * rt
                k0 = pl.multiple_of(tokens + row0 + rt - span, rt)
                k = k_win[pl.ds(k0, span), :]
                v = v_win[pl.ds(k0, span), :]
                mask = jnp.concatenate([bias[r, tokens + rt - span :, :]] * HEADS_STEP, axis=1)
                dk = dv = None
                for h in range(0, G, HEADS_STEP):
                    heads = [slice((h + i) * HD, (h + i + 1) * HD) for i in range(HEADS_STEP)]
                    rows = pl.ds(row0, rt)
                    q = jnp.concatenate([q_ref[rows, s] for s in heads], axis=0)
                    do = jnp.concatenate([do_ref[rows, s] for s in heads], axis=0)
                    s = lax.dot_general(k, q, NT, preferred_element_type=F32) + mask
                    dp = lax.dot_general(v, do, NT, preferred_element_type=F32)
                    e = jnp.exp2((s - jnp.max(s, axis=0, keepdims=True)) * scale)
                    inv = 1.0 / jnp.sum(e, axis=0, keepdims=True)
                    delta = jnp.sum(e * dp, axis=0, keepdims=True) * inv
                    p = e * inv
                    ds = (p * (dp - delta)).astype(BF16)
                    dv_h = lax.dot_general(p.astype(BF16), do, NN, preferred_element_type=F32)
                    dk_h = lax.dot_general(ds, q, NN, preferred_element_type=F32)
                    dk = dk_h if dk is None else dk + dk_h
                    dv = dv_h if dv is None else dv + dv_h
                    dq = lax.dot_general(ds, k, TN, preferred_element_type=F32)
                    dq = (dq * factor).astype(BF16)
                    for i, s in enumerate(heads):
                        dq_ref[rows, s] = dq[i * rt : (i + 1) * rt]
                dk_acc[pl.ds(k0, span), :] += dk
                dv_acc[pl.ds(k0, span), :] += dv

        return 0

    lax.fori_loop(0, n_tiles, row_tile, 0)
    for place, dk, dv in zip(places, dk_out, dv_out):
        dk[...] = (dk_acc[pl.ds(place, part), :] * factor).astype(dk.dtype)
        dv[...] = dv_acc[pl.ds(place, part), :].astype(dv.dtype)


def attention(info, docs, queries, grad_output, prev, own, grad_queries, chunk):
    tokens = queries.shape[0]
    pieces = len(own)
    part = tokens // pieces
    width = own[0].shape[1] // 2
    heads = width // HD
    first = chunk * heads
    wide = pl.BlockSpec((tokens, G * HD), lambda k: (0, first + k))
    key_block = pl.BlockSpec((part, HD), lambda k: (0, k))
    val_block = pl.BlockSpec((part, HD), lambda k: (0, heads + k))
    scalars = pl.BlockSpec(memory_space=pltpu.SMEM)
    count = 2 * pieces
    aliased = grad_queries is not None
    narrow = [jax.ShapeDtypeStruct((part, width), BF16)] * pieces + [
        jax.ShapeDtypeStruct((part, width), F32)
    ] * pieces
    work = 2 * tokens * G * HD * tokens * heads
    outs = pl.pallas_call(
        functools.partial(attn_kernel, tokens=tokens, pieces=pieces, aliased=aliased),
        grid=(heads,),
        in_specs=[scalars, scalars, wide, wide]
        + [key_block] * count
        + [val_block] * count
        + ([pl.BlockSpec(memory_space=pl.ANY)] if aliased else []),
        out_specs=[wide] + [key_block] * (2 * count),
        out_shape=[jax.ShapeDtypeStruct(queries.shape, BF16)] + narrow + narrow,
        scratch_shapes=[pltpu.VMEM((2 * tokens, HD), BF16)] * 2
        + [pltpu.VMEM((2 * tokens, HD), F32)] * 2
        + [
            pltpu.VMEM((tokens // ROW_TILE, tokens + ROW_TILE, ROW_TILE), F32),
            pltpu.SMEM((tokens // ROW_TILE,), jnp.int32),
        ],
        input_output_aliases={4 + 2 * count: 0} if aliased else {},
        compiler_params=pltpu.CompilerParams(vmem_limit_bytes=40 << 20),
        cost_estimate=pl.CostEstimate(
            flops=5 * work, bytes_accessed=3 * tokens * G * HD * 2 * heads, transcendentals=0
        ),
        name="attention",
    )(info, docs, queries, grad_output, *(prev + own) * 2, *([grad_queries] if aliased else []))
    dq, rest = outs[0], outs[1:]
    dk, dv = rest[:count], rest[count:]
    join = lambda i: jnp.concatenate([dk[i], dv[i]], axis=1)
    pair = lambda i: (dk[i], dv[i])
    return dq, [join(i) for i in range(pieces)], [pair(i) for i in range(pieces, count)]


def shift(value, steps):
    count = lax.axis_size("ctx")
    first, last = max(0, -steps), min(count, count - steps)
    return lax.ppermute(value, "ctx", [(i, i + steps) for i in range(first, last)])


def swap(value):
    return lax.ppermute(value, "head", [(0, 1), (1, 0)])


def add(own, arrived):
    return (jnp.concatenate(own, axis=1) + arrived.astype(F32)).astype(BF16)


def per_device(queries, key_rows, value_rows, grad_output, doc_lengths):
    tokens = queries.shape[0]
    head_count = lax.axis_size("head")
    kv_local = KVH // head_count
    local = kv_local * HD
    me = lax.axis_index("head")
    shard = lax.axis_index("ctx")
    chunks = 2 if kv_local % 2 == 0 else 1
    width = local // chunks
    cut = lambda x, start: lax.dynamic_slice_in_dim(x, start, width, axis=1)
    grad_queries = None

    if head_count == 2:
        info = jnp.stack([shard, me * (tokens // 2)]).astype(jnp.int32)
        both = lambda start: jnp.concatenate([cut(key_rows, start), cut(value_rows, start)], axis=1)
        mine = [both(me * local + j * width) for j in range(chunks)]
        recv = [swap(both((1 - me) * local + j * width)) for j in range(chunks)]
        prev = [[shift(mine[j], 1), shift(recv[j], 1)] for j in range(chunks)]
        kept, taken = [], []
        for j in range(chunks):
            grad_queries, gone, own = attention(
                info, doc_lengths, queries, grad_output, prev[j], [mine[j], recv[j]], grad_queries, j
            )
            taken.append(swap(add(own[1], shift(gone[1], -1))))
            kept.append(add(own[0], shift(gone[0], -1)))
        outs = []
        for at in range(2):
            here = [x[:, at * width : (at + 1) * width] for x in kept]
            there = [x[:, at * width : (at + 1) * width] for x in taken]
            low = jnp.concatenate([jnp.where(me == 0, a, b) for a, b in zip(here, there)], axis=1)
            high = jnp.concatenate([jnp.where(me == 0, b, a) for a, b in zip(here, there)], axis=1)
            outs.append(jnp.concatenate([low, high], axis=1))
        return (grad_queries, *outs)

    info = jnp.stack([shard, 0 * shard]).astype(jnp.int32)
    key_own = lax.all_to_all(key_rows, "head", split_axis=1, concat_axis=0, tiled=True)
    val_own = lax.all_to_all(value_rows, "head", split_axis=1, concat_axis=0, tiled=True)
    totals = []
    for j in range(chunks):
        own = jnp.concatenate([cut(key_own, j * width), cut(val_own, j * width)], axis=1)
        grad_queries, gone, mine = attention(
            info, doc_lengths, queries, grad_output, [shift(own, 1)], [own], grad_queries, j
        )
        totals.append(add(mine[0], shift(gone[0], -1)))
    outs = []
    for at in range(2):
        total = jnp.concatenate([x[:, at * width : (at + 1) * width] for x in totals], axis=1)
        outs.append(lax.all_to_all(total, "head", split_axis=0, concat_axis=1, tiled=True))
    return (grad_queries, *outs)


def solution(mesh):
    in_specs = (
        P("ctx", "head"),
        P(("ctx", "head"), None),
        P(("ctx", "head"), None),
        P("ctx", "head"),
        P(),
    )
    out_specs = (P("ctx", "head"), P(("ctx", "head"), None), P(("ctx", "head"), None))
    return jax.shard_map(
        per_device, mesh=mesh, in_specs=in_specs, out_specs=out_specs, check_vma=False
    )
```

time: 266 us -> 97.3 us (0.37)
  the two profiles are of different devices: /device:TPU:15 before, /device:TPU:18 now
where the time goes in v1:
time: 97.3 us; the launch traced here: 96.6 us
  Pallas kernels  40.7 us (42%)
  starting transfers between devices  30.7 us (32%)
  waiting for transfers between devices  16.3 us (17%)
  local copies, waits for them, and re-layouts  5.76 us (6%)
  other arithmetic  2.24 us (2%)
    pallas_call x2, Pallas kernels, attention(): pl.pallas_call(functools.partial(attn_kernel, tokens=tokens, pieces=piece...  40.7 us
    ppermute x8, starting transfers between devices, shift(): lax.ppermute(value, 'ctx', [(i, i + steps) for i in range(first, last)])  25.4 us
    ppermute x4, waiting for transfers between devices, swap(): return lax.ppermute(value, 'head', [(0, 1), (1, 0)])  14.8 us
    ppermute x4, starting transfers between devices, swap(): return lax.ppermute(value, 'head', [(0, 1), (1, 0)])  5.32 us
    unnamed x6, local copies, waits for them, and re-layouts  4.38 us
  transfers between devices with their start and end apart: 12, of which 6 were waited for; matrix products, arithmetic and copies ran while one was open for 0% of the time, Pallas kernels for 42%

profile of v1, /device:TPU:18, one launch (start us, length us, event | category | flops | bytes accessed | tf_op | source)
XLA Modules:
  0.0 96.6 jit_solution(13818472141555317497)
XLA Ops:
  0.6 0.0 copy-start.2
  0.6 1.4 %constant_dynamic-slice_fusion = (bf16[256,256]{1,0:T(8,128)(2,1)S(1)}, bf16[256,256]{1,0:T(8,128)(2,1)S(1)}, bf16[256,256]{1,0:T(8,128)(2,1)S(1)}, bf16[256,256...) fusion(bf16[256,1024]{1,0:T(8,128)(2,1)} %param.7, ...), kind=kLoop, calls=%fused_computation.26 | loop fusion | bytes 2097168 | tf_op jit(solution)/shard_map/dynamic_slice | solution.py:190
  2.1 1.6 %collective-permute-start.4 = (bf16[256,512]{1,0:T(8,128)(2,1)S(1)}, bf16[256,512]{1,0:T(8,128)(2,1)S(1)}, u32[]{:S(2)}, u32[]{:S(2)}) collective-permute-start(bf16[256,512]{1,0:T(8,128)(2,1)S(1)} %pad_maximum_fusion.5), channel_id=1, source_target_pairs={{0,1},{1,0},{2,3},{3,2},{4,5},{5,4},{6,7},{7,6},{8,9},{9,8},{10,11... | collective-permute-start | bytes 786440 | tf_op jit(solution)/shard_map/ppermute | solution.py:174
  3.7 0.6 collective-permute-start.1
  4.3 1.9 %collective-permute-start.3 = (bf16[256,512]{1,0:T(8,128)(2,1)S(1)}, bf16[256,512]{1,0:T(8,128)(2,1)S(1)}, u32[]{:S(2)}, u32[]{:S(2)}) collective-permute-start(bf16[256,512]{1,0:T(8,128)(2,1)S(1)} %pad_maximum_fusion.4.refs_2_.refs_6_), channel_id=1, source_target_pairs={{0,2},{2,4},{4,6},{6,8},{8,10},{10,12},{12,14},{14,16},{16,18},{18... | collective-permute-start | bytes 786440 | tf_op jit(solution)/shard_map/ppermute | solution.py:170
  6.2 5.1 %collective-permute-done.4.refs_3_.refs_7_ = bf16[256,512]{1,0:T(8,128)(2,1)S(1)} collective-permute-done((bf16[256,512]{1,0:T(8,128)(2,1)S(1)}, bf16[256,512]{1,0:T(8,128)(2,1)S(1)}, u32[]{:S(2)}, u32[]{:S(2)}) %collective-permute-start.4) | collective-permute-done | bytes 262176 | tf_op jit(solution)/shard_map/ppermute | solution.py:174
  11.3 1.9 %collective-permute-start.5 = (bf16[256,512]{1,0:T(8,128)(2,1)S(1)}, bf16[256,512]{1,0:T(8,128)(2,1)S(1)}, u32[]{:S(2)}, u32[]{:S(2)}) collective-permute-start(bf16[256,512]{1,0:T(8,128)(2,1)S(1)} %collective-permute-done.4.refs_3_.refs_7_), channel_id=1, source_target_pairs={{0,2},{2,4},{4,6},{6,8},{8,10},{10,12},{12,14},{14,16},{16,18},{18... | collective-permute-start | bytes 786440 | tf_op jit(solution)/shard_map/ppermute | solution.py:170
  13.3 3.6 %collective-permute-start = (bf16[256,512]{1,0:T(8,128)(2,1)S(1)}, bf16[256,512]{1,0:T(8,128)(2,1)S(1)}, u32[]{:S(2)}, u32[]{:S(2)}) collective-permute-start(bf16[256,512]{1,0:T(8,128)(2,1)S(1)} %pad_maximum_fusion.2.refs_2_.refs_6_), channel_id=1, source_target_pairs={{0,2},{2,4},{4,6},{6,8},{8,10},{10,12},{12,14},{14,16},{16,18},{18... | collective-permute-start | bytes 786440 | tf_op jit(solution)/shard_map/ppermute | solution.py:170
  16.8 0.1 pad_add_fusion.info_ref
  16.9 0.0 collective-permute-done.1.refs_3_.refs_7_
  16.9 1.9 %collective-permute-start.2 = (bf16[256,512]{1,0:T(8,128)(2,1)S(1)}, bf16[256,512]{1,0:T(8,128)(2,1)S(1)}, u32[]{:S(2)}, u32[]{:S(2)}) collective-permute-start(bf16[256,512]{1,0:T(8,128)(2,1)S(1)} %collective-permute-done.1.refs_3_.refs_7_), channel_id=1, source_target_pairs={{0,2},{2,4},{4,6},{6,8},{8,10},{10,12},{12,14},{14,16},{16,18},{18... | collective-permute-start | bytes 786440 | tf_op jit(solution)/shard_map/ppermute | solution.py:170
  18.8 0.0 collective-permute-done.3.refs_0_.refs_4_
  18.8 0.2 collective-permute-done.5.refs_1_.refs_5_
  19.0 0.0 copy-done.2
  19.0 0.0 copy-start
  19.0 2.2 %copy-done = bf16[512,4096]{1,0:T(8,128)(2,1)S(1)} copy-done((bf16[512,4096]{1,0:T(8,128)(2,1)S(1)}, bf16[512,4096]{1,0:T(8,128)(2,1)}, u32[]{:S(2)}) %copy-start) | copy-done | bytes 4194328
  21.2 0.0 copy-start.1
  21.2 2.2 %copy-done.1 = bf16[512,4096]{1,0:T(8,128)(2,1)S(1)} copy-done((bf16[512,4096]{1,0:T(8,128)(2,1)S(1)}, bf16[512,4096]{1,0:T(8,128)(2,1)}, u32[]{:S(2)}) %copy-start.1) | copy-done | bytes 4194328
  23.4 20.3 %attention.2 = (bf16[512,4096]{1,0:T(8,128)(2,1)}, bf16[256,256]{1,0:T(8,128)(2,1)S(1)}, bf16[256,256]{1,0:T(8,128)(2,1)S(1)}, f32[256,256]{1,0:T(8,128)S(1)}, f...) custom-call(s32[2]{0:T(128)S(1)} %pad_add_fusion.info_ref, ...), custom_call_target="tpu_custom_call" | custom-call | flops 5368709120 | bytes 6291456 | tf_op jit(solution)/shard_map/attention/pallas_call | solution.py:138
  43.7 6.6 %collective-permute-start.7 = (bf16[256,512]{1,0:T(8,128)(2,1)S(1)}, bf16[256,512]{1,0:T(8,128)(2,1)S(1)}, u32[]{:S(2)}, u32[]{:S(2)}) collective-permute-start(bf16[256,512]{1,0:T(8,128)(2,1)S(1)} %pad_maximum_fusion.7), channel_id=1, source_target_pairs={{2,0},{4,2},{6,4},{8,6},{10,8},{12,10},{14,12},{16,14},{18,16},{20... | collective-permute-start | bytes 786440 | tf_op jit(solution)/shard_map/ppermute | solution.py:170
  50.4 2.1 %collective-permute-start.6 = (bf16[256,512]{1,0:T(8,128)(2,1)S(1)}, bf16[256,512]{1,0:T(8,128)(2,1)S(1)}, u32[]{:S(2)}, u32[]{:S(2)}) collective-permute-start(bf16[256,512]{1,0:T(8,128)(2,1)S(1)} %pad_maximum_fusion.6), channel_id=1, source_target_pairs={{2,0},{4,2},{6,4},{8,6},{10,8},{12,10},{14,12},{16,14},{18,16},{20... | collective-permute-start | bytes 786440 | tf_op jit(solution)/shard_map/ppermute | solution.py:170
  52.5 0.0 collective-permute-done.refs_0_.refs_4_
  52.5 0.0 collective-permute-done.2.refs_1_.refs_5_
  52.5 20.4 %attention.3 = (bf16[512,4096]{1,0:T(8,128)(2,1)}, bf16[256,256]{1,0:T(8,128)(2,1)S(1)}, bf16[256,256]{1,0:T(8,128)(2,1)S(1)}, f32[256,256]{1,0:T(8,128)S(1)}, f...) custom-call(s32[2]{0:T(128)S(1)} %pad_add_fusion.info_ref, ...), custom_call_target="tpu_custom_call", output_to_operand_aliasing={{0}: (12, {})} | custom-call | flops 5368709120 | bytes 6291456 | tf_op jit(solution)/shard_map/attention/pallas_call | solution.py:138
  72.9 5.5 %collective-permute-start.10 = (bf16[256,512]{1,0:T(8,128)(2,1)S(1)}, bf16[256,512]{1,0:T(8,128)(2,1)S(1)}, u32[]{:S(2)}, u32[]{:S(2)}) collective-permute-start(bf16[256,512]{1,0:T(8,128)(2,1)S(1)} %pad_maximum_fusion.9), channel_id=1, source_target_pairs={{2,0},{4,2},{6,4},{8,6},{10,8},{12,10},{14,12},{16,14},{18,16},{20... | collective-permute-start | bytes 786440 | tf_op jit(solution)/shard_map/ppermute | solution.py:170
  78.4 1.9 %collective-permute-start.9 = (bf16[256,512]{1,0:T(8,128)(2,1)S(1)}, bf16[256,512]{1,0:T(8,128)(2,1)S(1)}, u32[]{:S(2)}, u32[]{:S(2)}) collective-permute-start(bf16[256,512]{1,0:T(8,128)(2,1)S(1)} %pad_maximum_fusion.8), channel_id=1, source_target_pairs={{2,0},{4,2},{6,4},{8,6},{10,8},{12,10},{14,12},{16,14},{18,16},{20... | collective-permute-start | bytes 786440 | tf_op jit(solution)/shard_map/ppermute | solution.py:170
  80.3 0.0 collective-permute-done.7
  80.4 0.1 fusion.1
  80.4 1.6 %collective-permute-start.8 = (bf16[256,512]{1,0:T(8,128)(2,1)S(1)}, bf16[256,512]{1,0:T(8,128)(2,1)S(1)}, u32[]{:S(2)}, u32[]{:S(2)}) collective-permute-start(bf16[256,512]{1,0:T(8,128)(2,1)S(1)} %fusion.1), channel_id=1, source_target_pairs={{0,1},{1,0},{2,3},{3,2},{4,5},{5,4},{6,7},{7,6},{8,9},{9,8},{10,11... | collective-permute-start | bytes 786440 | tf_op jit(solution)/shard_map/ppermute | solution.py:174
  82.0 0.3 collective-permute-done.10
  82.3 0.1 fusion.3
  82.3 1.6 %collective-permute-start.11 = (bf16[256,512]{1,0:T(8,128)(2,1)S(1)}, bf16[256,512]{1,0:T(8,128)(2,1)S(1)}, u32[]{:S(2)}, u32[]{:S(2)}) collective-permute-start(bf16[256,512]{1,0:T(8,128)(2,1)S(1)} %fusion.3), channel_id=1, source_target_pairs={{0,1},{1,0},{2,3},{3,2},{4,5},{5,4},{6,7},{7,6},{8,9},{9,8},{10,11... | collective-permute-start | bytes 786440 | tf_op jit(solution)/shard_map/ppermute | solution.py:174
  83.9 0.0 collective-permute-done.6
  83.9 0.1 fusion
  84.0 1.1 %collective-permute-done.9 = bf16[256,512]{1,0:T(8,128)(2,1)S(1)} collective-permute-done((bf16[256,512]{1,0:T(8,128)(2,1)S(1)}, bf16[256,512]{1,0:T(8,128)(2,1)S(1)}, u32[]{:S(2)}, u32[]{:S(2)}) %collective-permute-start.9) | collective-permute-done | bytes 262176 | tf_op jit(solution)/shard_map/ppermute | solution.py:170
  85.1 0.1 fusion.2
  85.1 4.5 %collective-permute-done.8 = bf16[256,512]{1,0:T(8,128)(2,1)S(1)} collective-permute-done((bf16[256,512]{1,0:T(8,128)(2,1)S(1)}, bf16[256,512]{1,0:T(8,128)(2,1)S(1)}, u32[]{:S(2)}, u32[]{:S(2)}) %collective-permute-start.8) | collective-permute-done | bytes 262176 | tf_op jit(solution)/shard_map/ppermute | solution.py:174
  89.6 5.2 %collective-permute-done.11 = bf16[256,512]{1,0:T(8,128)(2,1)S(1)} collective-permute-done((bf16[256,512]{1,0:T(8,128)(2,1)S(1)}, bf16[256,512]{1,0:T(8,128)(2,1)S(1)}, u32[]{:S(2)}, u32[]{:S(2)}) %collective-permute-start.11) | collective-permute-done | bytes 262176 | tf_op jit(solution)/shard_map/ppermute | solution.py:174
  94.8 0.9 pad_maximum_fusion.1
  95.7 0.9 pad_maximum_fusion
  (10 shorter events, 0.2 us)
Async XLA Ops:
  0.6 18.4 %copy-start.2 = (s32[32]{0:T(128)S(1)}, s32[32]{0:T(128)}, u32[]{:S(2)}) copy-start(s32[32]{0:T(128)} %docs_ref.3) | copy-start | bytes 388
  2.1 9.3 %collective-permute-start.4 = (bf16[256,512]{1,0:T(8,128)(2,1)S(1)}, bf16[256,512]{1,0:T(8,128)(2,1)S(1)}, u32[]{:S(2)}, u32[]{:S(2)}) collective-permute-start(bf16[256,512]{1,0:T(8,128)(2,1)S(1)} %pad_maximum_fusion.5), channel_id=1, source_target_pairs={{0,1},{1,0},{2,3},{3,2},{4,5},{5,4},{6,7},{7,6},{8,9},{9,8},{10,11... | collective-permute-start | bytes 786440 | tf_op jit(solution)/shard_map/ppermute | solution.py:174
  3.7 13.3 %collective-permute-start.1 = (bf16[256,512]{1,0:T(8,128)(2,1)S(1)}, bf16[256,512]{1,0:T(8,128)(2,1)S(1)}, u32[]{:S(2)}, u32[]{:S(2)}) collective-permute-start(bf16[256,512]{1,0:T(8,128)(2,1)S(1)} %pad_maximum_fusion.3), channel_id=1, source_target_pairs={{0,1},{1,0},{2,3},{3,2},{4,5},{5,4},{6,7},{7,6},{8,9},{9,8},{10,11... | collective-permute-start | bytes 786440 | tf_op jit(solution)/shard_map/ppermute | solution.py:174
  4.3 14.6 %collective-permute-start.3 = (bf16[256,512]{1,0:T(8,128)(2,1)S(1)}, bf16[256,512]{1,0:T(8,128)(2,1)S(1)}, u32[]{:S(2)}, u32[]{:S(2)}) collective-permute-start(bf16[256,512]{1,0:T(8,128)(2,1)S(1)} %pad_maximum_fusion.4.refs_2_.refs_6_), channel_id=1, source_target_pairs={{0,2},{2,4},{4,6},{6,8},{8,10},{10,12},{12,14},{14,16},{16,18},{18... | collective-permute-start | bytes 786440 | tf_op jit(solution)/shard_map/ppermute | solution.py:170
  11.3 7.7 %collective-permute-start.5 = (bf16[256,512]{1,0:T(8,128)(2,1)S(1)}, bf16[256,512]{1,0:T(8,128)(2,1)S(1)}, u32[]{:S(2)}, u32[]{:S(2)}) collective-permute-start(bf16[256,512]{1,0:T(8,128)(2,1)S(1)} %collective-permute-done.4.refs_3_.refs_7_), channel_id=1, source_target_pairs={{0,2},{2,4},{4,6},{6,8},{8,10},{10,12},{12,14},{14,16},{16,18},{18... | collective-permute-start | bytes 786440 | tf_op jit(solution)/shard_map/ppermute | solution.py:170
  13.3 39.2 %collective-permute-start = (bf16[256,512]{1,0:T(8,128)(2,1)S(1)}, bf16[256,512]{1,0:T(8,128)(2,1)S(1)}, u32[]{:S(2)}, u32[]{:S(2)}) collective-permute-start(bf16[256,512]{1,0:T(8,128)(2,1)S(1)} %pad_maximum_fusion.2.refs_2_.refs_6_), channel_id=1, source_target_pairs={{0,2},{2,4},{4,6},{6,8},{8,10},{10,12},{12,14},{14,16},{16,18},{18... | collective-permute-start | bytes 786440 | tf_op jit(solution)/shard_map/ppermute | solution.py:170
  16.9 35.6 %collective-permute-start.2 = (bf16[256,512]{1,0:T(8,128)(2,1)S(1)}, bf16[256,512]{1,0:T(8,128)(2,1)S(1)}, u32[]{:S(2)}, u32[]{:S(2)}) collective-permute-start(bf16[256,512]{1,0:T(8,128)(2,1)S(1)} %collective-permute-done.1.refs_3_.refs_7_), channel_id=1, source_target_pairs={{0,2},{2,4},{4,6},{6,8},{8,10},{10,12},{12,14},{14,16},{16,18},{18... | collective-permute-start | bytes 786440 | tf_op jit(solution)/shard_map/ppermute | solution.py:170
  19.0 2.2 %copy-start = (bf16[512,4096]{1,0:T(8,128)(2,1)S(1)}, bf16[512,4096]{1,0:T(8,128)(2,1)}, u32[]{:S(2)}) copy-start(bf16[512,4096]{1,0:T(8,128)(2,1)} %q_ref.3) | copy-start | bytes 12582916
  21.2 2.2 %copy-start.1 = (bf16[512,4096]{1,0:T(8,128)(2,1)S(1)}, bf16[512,4096]{1,0:T(8,128)(2,1)}, u32[]{:S(2)}) copy-start(bf16[512,4096]{1,0:T(8,128)(2,1)} %do_ref.3) | copy-start | bytes 12582916
  43.7 36.6 %collective-permute-start.7 = (bf16[256,512]{1,0:T(8,128)(2,1)S(1)}, bf16[256,512]{1,0:T(8,128)(2,1)S(1)}, u32[]{:S(2)}, u32[]{:S(2)}) collective-permute-start(bf16[256,512]{1,0:T(8,128)(2,1)S(1)} %pad_maximum_fusion.7), channel_id=1, source_target_pairs={{2,0},{4,2},{6,4},{8,6},{10,8},{12,10},{14,12},{16,14},{18,16},{20... | collective-permute-start | bytes 786440 | tf_op jit(solution)/shard_map/ppermute | solution.py:170
  50.4 33.5 %collective-permute-start.6 = (bf16[256,512]{1,0:T(8,128)(2,1)S(1)}, bf16[256,512]{1,0:T(8,128)(2,1)S(1)}, u32[]{:S(2)}, u32[]{:S(2)}) collective-permute-start(bf16[256,512]{1,0:T(8,128)(2,1)S(1)} %pad_maximum_fusion.6), channel_id=1, source_target_pairs={{2,0},{4,2},{6,4},{8,6},{10,8},{12,10},{14,12},{16,14},{18,16},{20... | collective-permute-start | bytes 786440 | tf_op jit(solution)/shard_map/ppermute | solution.py:170
  72.9 9.4 %collective-permute-start.10 = (bf16[256,512]{1,0:T(8,128)(2,1)S(1)}, bf16[256,512]{1,0:T(8,128)(2,1)S(1)}, u32[]{:S(2)}, u32[]{:S(2)}) collective-permute-start(bf16[256,512]{1,0:T(8,128)(2,1)S(1)} %pad_maximum_fusion.9), channel_id=1, source_target_pairs={{2,0},{4,2},{6,4},{8,6},{10,8},{12,10},{14,12},{16,14},{18,16},{20... | collective-permute-start | bytes 786440 | tf_op jit(solution)/shard_map/ppermute | solution.py:170
  78.4 6.7 %collective-permute-start.9 = (bf16[256,512]{1,0:T(8,128)(2,1)S(1)}, bf16[256,512]{1,0:T(8,128)(2,1)S(1)}, u32[]{:S(2)}, u32[]{:S(2)}) collective-permute-start(bf16[256,512]{1,0:T(8,128)(2,1)S(1)} %pad_maximum_fusion.8), channel_id=1, source_target_pairs={{2,0},{4,2},{6,4},{8,6},{10,8},{12,10},{14,12},{16,14},{18,16},{20... | collective-permute-start | bytes 786440 | tf_op jit(solution)/shard_map/ppermute | solution.py:170
  80.4 9.2 %collective-permute-start.8 = (bf16[256,512]{1,0:T(8,128)(2,1)S(1)}, bf16[256,512]{1,0:T(8,128)(2,1)S(1)}, u32[]{:S(2)}, u32[]{:S(2)}) collective-permute-start(bf16[256,512]{1,0:T(8,128)(2,1)S(1)} %fusion.1), channel_id=1, source_target_pairs={{0,1},{1,0},{2,3},{3,2},{4,5},{5,4},{6,7},{7,6},{8,9},{9,8},{10,11... | collective-permute-start | bytes 786440 | tf_op jit(solution)/shard_map/ppermute | solution.py:174
  82.3 12.5 %collective-permute-start.11 = (bf16[256,512]{1,0:T(8,128)(2,1)S(1)}, bf16[256,512]{1,0:T(8,128)(2,1)S(1)}, u32[]{:S(2)}, u32[]{:S(2)}) collective-permute-start(bf16[256,512]{1,0:T(8,128)(2,1)S(1)} %fusion.3), channel_id=1, source_target_pairs={{0,1},{1,0},{2,3},{3,2},{4,5},{5,4},{6,7},{7,6},{8,9},{9,8},{10,11... | collective-permute-start | bytes 786440 | tf_op jit(solution)/shard_map/ppermute | solution.py:174

commit v2 on v1

--- a/solution.py
+++ b/solution.py
@@ -14,7 +14,7 @@
 G = H // KVH
 NEG = -1e30
 ROW_TILE = 128
-HEADS_STEP = 2
+HEADS_STEP = 8
 BF16 = jnp.bfloat16
 F32 = jnp.float32
 NT = (((1,), (1,)), ((), ()))
@@ -151,7 +151,7 @@
             pltpu.SMEM((tokens // ROW_TILE,), jnp.int32),
         ],
         input_output_aliases={4 + 2 * count: 0} if aliased else {},
-        compiler_params=pltpu.CompilerParams(vmem_limit_bytes=40 << 20),
+        compiler_params=pltpu.CompilerParams(vmem_limit_bytes=51 << 20),
         cost_estimate=pl.CostEstimate(
             flops=5 * work, bytes_accessed=3 * tokens * G * HD * 2 * heads, transcendentals=0
         ),
@@ -195,14 +195,22 @@
         both = lambda start: jnp.concatenate([cut(key_rows, start), cut(value_rows, start)], axis=1)
         mine = [both(me * local + j * width) for j in range(chunks)]
         recv = [swap(both((1 - me) * local + j * width)) for j in range(chunks)]
-        prev = [[shift(mine[j], 1), shift(recv[j], 1)] for j in range(chunks)]
+        prev = [[shift(mine[0], 1), shift(recv[0], 1)]]
+        for j in range(1, chunks):
+            arrived = shift(jnp.concatenate([mine[j], recv[j]], axis=0), 1)
+            prev.append([arrived[: tokens // 2], arrived[tokens // 2 :]])
         kept, taken = [], []
         for j in range(chunks):
             grad_queries, gone, own = attention(
                 info, doc_lengths, queries, grad_output, prev[j], [mine[j], recv[j]], grad_queries, j
             )
-            taken.append(swap(add(own[1], shift(gone[1], -1))))
-            kept.append(add(own[0], shift(gone[0], -1)))
+            if j < chunks - 1:
+                back = shift(jnp.concatenate(gone, axis=0), -1)
+                back = [back[: tokens // 2], back[tokens // 2 :]]
+            else:
+                back = [shift(x, -1) for x in gone]
+            taken.append(swap(add(own[1], back[1])))
+            kept.append(add(own[0], back[0]))
         outs = []
         for at in range(2):
             here = [x[:, at * width : (at + 1) * width] for x in kept]

time: 97.3 us -> 80.9 us (0.83)
  the two profiles are of different devices: /device:TPU:18 before, /device:TPU:15 now
where the time goes in v2:
time: 80.9 us
  Pallas kernels  32.4 us (40%)
  starting transfers between devices  30.8 us (38%)
  waiting for transfers between devices  13.2 us (16%)
  other arithmetic  2.28 us (3%)
  local copies, waits for them, and re-layouts  1.42 us (2%)
  between operations  0.83 us (1%)
    pallas_call x2, Pallas kernels, attention(): pl.pallas_call(functools.partial(attn_kernel, tokens=tokens, pieces=piece...  32.4 us
    ppermute x6, starting transfers between devices, shift(): lax.ppermute(value, 'ctx', [(i, i + steps) for i in range(first, last)])  27.6 us
    ppermute x4, waiting for transfers between devices, swap(): return lax.ppermute(value, 'head', [(0, 1), (1, 0)])  13.1 us
    ppermute x4, starting transfers between devices, swap(): return lax.ppermute(value, 'head', [(0, 1), (1, 0)])  3.19 us
    concatenate x2, other arithmetic, per_device(): outs.append(jnp.concatenate([low, high], axis=1))  1.72 us
  transfers between devices with their start and end apart: 10, of which 3 were waited for; matrix products, arithmetic and copies ran while one was open for 1% of the time, Pallas kernels for 40%

profile of v2, /device:TPU:15, one launch (start us, length us, event | category | flops | bytes accessed | tf_op | source)
XLA Modules:
  0.0 80.9 jit_solution(10061905174126886925)
XLA Ops:
  0.6 0.0 copy-start
  0.6 1.4 %constant_dynamic-slice_fusion = (bf16[256,256]{1,0:T(8,128)(2,1)S(1)}, bf16[256,256]{1,0:T(8,128)(2,1)S(1)}, bf16[256,256]{1,0:T(8,128)(2,1)S(1)}, bf16[256,256...) fusion(bf16[256,1024]{1,0:T(8,128)(2,1)} %param.7, ...), kind=kLoop, calls=%fused_computation.26 | loop fusion | bytes 2097168 | tf_op jit(solution)/shard_map/dynamic_slice | solution.py:190
  2.1 0.3 collective-permute-start.3
  2.4 1.3 %collective-permute-start = (bf16[256,512]{1,0:T(8,128)(2,1)S(1)}, bf16[256,512]{1,0:T(8,128)(2,1)S(1)}, u32[]{:S(2)}, u32[]{:S(2)}) collective-permute-start(bf16[256,512]{1,0:T(8,128)(2,1)S(1)} %pad_maximum_fusion.4), channel_id=1, source_target_pairs={{0,1},{1,0},{2,3},{3,2},{4,5},{5,4},{6,7},{7,6},{8,9},{9,8},{10,11... | collective-permute-start | bytes 786440 | tf_op jit(solution)/shard_map/ppermute | solution.py:174
  3.7 4.3 %collective-permute-start.2 = (bf16[256,512]{1,0:T(8,128)(2,1)S(1)}, bf16[256,512]{1,0:T(8,128)(2,1)S(1)}, u32[]{:S(2)}, u32[]{:S(2)}) collective-permute-start(bf16[256,512]{1,0:T(8,128)(2,1)S(1)} %pad_maximum_fusion.5.refs_2_.refs_6_), channel_id=1, source_target_pairs={{0,2},{2,4},{4,6},{6,8},{8,10},{10,12},{12,14},{14,16},{16,18},{18... | collective-permute-start | bytes 786440 | tf_op jit(solution)/shard_map/ppermute | solution.py:170
  8.0 1.3 %collective-permute-done.3.refs_3_.refs_7_ = bf16[256,512]{1,0:T(8,128)(2,1)S(1)} collective-permute-done((bf16[256,512]{1,0:T(8,128)(2,1)S(1)}, bf16[256,512]{1,0:T(8,128)(2,1)S(1)}, u32[]{:S(2)}, u32[]{:S(2)}) %collective-permute-start.3) | collective-permute-done | bytes 262176 | tf_op jit(solution)/shard_map/ppermute | solution.py:174
  9.3 5.7 %collective-permute-start.4 = (bf16[256,512]{1,0:T(8,128)(2,1)S(1)}, bf16[256,512]{1,0:T(8,128)(2,1)S(1)}, u32[]{:S(2)}, u32[]{:S(2)}) collective-permute-start(bf16[256,512]{1,0:T(8,128)(2,1)S(1)} %collective-permute-done.3.refs_3_.refs_7_), channel_id=1, source_target_pairs={{0,2},{2,4},{4,6},{6,8},{8,10},{10,12},{12,14},{14,16},{16,18},{18... | collective-permute-start | bytes 786440 | tf_op jit(solution)/shard_map/ppermute | solution.py:170
  15.0 0.1 pad_add_fusion.info_ref
  15.1 0.0 collective-permute-done.refs_3_.refs_7_
  15.2 4.4 %collective-permute-start.1 = (bf16[512,512]{1,0:T(8,128)(2,1)S(1)}, bf16[512,512]{1,0:T(8,128)(2,1)S(1)}, u32[]{:S(2)}, u32[]{:S(2)}) collective-permute-start(bf16[512,512]{1,0:T(8,128)(2,1)S(1)} %pad_maximum_fusion), channel_id=1, source_target_pairs={{0,2},{2,4},{4,6},{6,8},{8,10},{10,12},{12,14},{14,16},{16,18},{18... | collective-permute-start | bytes 1572872 | tf_op jit(solution)/shard_map/ppermute | solution.py:170
  19.6 0.0 collective-permute-done.2.refs_0_.refs_4_
  19.6 0.0 collective-permute-done.4.refs_1_.refs_5_
  19.6 0.0 copy-done
  19.6 16.2 %attention.2 = (bf16[512,4096]{1,0:T(8,128)(2,1)}, bf16[256,256]{1,0:T(8,128)(2,1)S(1)}, bf16[256,256]{1,0:T(8,128)(2,1)S(1)}, f32[256,256]{1,0:T(8,128)S(1)}, f...) custom-call(s32[2]{0:T(128)S(1)} %pad_add_fusion.info_ref, ...), custom_call_target="tpu_custom_call" | custom-call | flops 5368709120 | bytes 6291456 | tf_op jit(solution)/shard_map/attention/pallas_call | solution.py:138
  35.8 2.1 %collective-permute-start.5 = (bf16[512,512]{1,0:T(8,128)(2,1)S(1)}, bf16[512,512]{1,0:T(8,128)(2,1)S(1)}, u32[]{:S(2)}, u32[]{:S(2)}) collective-permute-start(bf16[512,512]{1,0:T(8,128)(2,1)S(1)} %maximum_maximum_fusion), channel_id=1, source_target_pairs={{2,0},{4,2},{6,4},{8,6},{10,8},{12,10},{14,12},{16,14},{18,16},{20... | collective-permute-start | bytes 1572872 | tf_op jit(solution)/shard_map/ppermute | solution.py:170
  37.9 0.0 collective-permute-done.1
  38.0 16.2 %attention.3 = (bf16[512,4096]{1,0:T(8,128)(2,1)}, bf16[256,256]{1,0:T(8,128)(2,1)S(1)}, bf16[256,256]{1,0:T(8,128)(2,1)S(1)}, f32[256,256]{1,0:T(8,128)S(1)}, f...) custom-call(s32[2]{0:T(128)S(1)} %pad_add_fusion.info_ref, ...), custom_call_target="tpu_custom_call", output_to_operand_aliasing={{0}: (12, {})} | custom-call | flops 5368709120 | bytes 6291456 | tf_op jit(solution)/shard_map/attention/pallas_call | solution.py:138
  54.2 3.3 %collective-permute-start.8 = (bf16[256,512]{1,0:T(8,128)(2,1)S(1)}, bf16[256,512]{1,0:T(8,128)(2,1)S(1)}, u32[]{:S(2)}, u32[]{:S(2)}) collective-permute-start(bf16[256,512]{1,0:T(8,128)(2,1)S(1)} %pad_maximum_fusion.8), channel_id=1, source_target_pairs={{2,0},{4,2},{6,4},{8,6},{10,8},{12,10},{14,12},{16,14},{18,16},{20... | collective-permute-start | bytes 786440 | tf_op jit(solution)/shard_map/ppermute | solution.py:170
  57.5 7.8 %collective-permute-start.7 = (bf16[256,512]{1,0:T(8,128)(2,1)S(1)}, bf16[256,512]{1,0:T(8,128)(2,1)S(1)}, u32[]{:S(2)}, u32[]{:S(2)}) collective-permute-start(bf16[256,512]{1,0:T(8,128)(2,1)S(1)} %pad_maximum_fusion.7), channel_id=1, source_target_pairs={{2,0},{4,2},{6,4},{8,6},{10,8},{12,10},{14,12},{16,14},{18,16},{20... | collective-permute-start | bytes 786440 | tf_op jit(solution)/shard_map/ppermute | solution.py:170
  65.3 0.0 collective-permute-done.5
  65.4 0.1 fusion
  65.5 0.3 collective-permute-start.6
  65.8 0.0 collective-permute-done.8
  65.8 0.1 fusion.3
  65.8 1.3 %collective-permute-start.9 = (bf16[256,512]{1,0:T(8,128)(2,1)S(1)}, bf16[256,512]{1,0:T(8,128)(2,1)S(1)}, u32[]{:S(2)}, u32[]{:S(2)}) collective-permute-start(bf16[256,512]{1,0:T(8,128)(2,1)S(1)} %fusion.3), channel_id=1, source_target_pairs={{0,1},{1,0},{2,3},{3,2},{4,5},{5,4},{6,7},{7,6},{8,9},{9,8},{10,11... | collective-permute-start | bytes 786440 | tf_op jit(solution)/shard_map/ppermute | solution.py:174
  67.1 0.0 collective-permute-done.7
  67.1 0.1 fusion.2
  67.2 6.3 %collective-permute-done.6 = bf16[256,512]{1,0:T(8,128)(2,1)S(1)} collective-permute-done((bf16[256,512]{1,0:T(8,128)(2,1)S(1)}, bf16[256,512]{1,0:T(8,128)(2,1)S(1)}, u32[]{:S(2)}, u32[]{:S(2)}) %collective-permute-start.6) | collective-permute-done | bytes 262176 | tf_op jit(solution)/shard_map/ppermute | solution.py:174
  73.5 5.6 %collective-permute-done.9 = bf16[256,512]{1,0:T(8,128)(2,1)S(1)} collective-permute-done((bf16[256,512]{1,0:T(8,128)(2,1)S(1)}, bf16[256,512]{1,0:T(8,128)(2,1)S(1)}, u32[]{:S(2)}, u32[]{:S(2)}) %collective-permute-start.9) | collective-permute-done | bytes 262176 | tf_op jit(solution)/shard_map/ppermute | solution.py:174
  79.1 0.9 %pad_maximum_fusion.2 = bf16[256,1024]{1,0:T(8,128)(2,1)} fusion(bf16[256,256]{1,0:T(8,128)(2,1)S(1)} %get-tuple-element.46, bf16[256,256]{1,0:T(8,128)(2,1)S(1)} %get-tuple-element.41, bf16[256,256]{1,0:T(8,128)(2,1)S(1)} %get-tuple-element.43, bf16[256,256]{1,0:T(8,128)(2,1)S(1)} %get-tuple-element.39), kind=kLoop, calls=%fused_computation.11 | loop fusion | flops 2097152 | bytes 1048576 | tf_op jit(solution)/shard_map/concatenate | solution.py:220
  80.0 0.9 %pad_maximum_fusion.1 = bf16[256,1024]{1,0:T(8,128)(2,1)} fusion(bf16[256,256]{1,0:T(8,128)(2,1)S(1)} %get-tuple-element.45, bf16[256,256]{1,0:T(8,128)(2,1)S(1)} %get-tuple-element.40, bf16[256,256]{1,0:T(8,128)(2,1)S(1)} %get-tuple-element.44, bf16[256,256]{1,0:T(8,128)(2,1)S(1)} %get-tuple-element.42), kind=kLoop, calls=%fused_computation.10 | loop fusion | flops 2097152 | bytes 1048576 | tf_op jit(solution)/shard_map/concatenate | solution.py:220
  (11 shorter events, 0.3 us)
Async XLA Ops:
  0.6 19.0 %copy-start = (s32[32]{0:T(128)S(1)}, s32[32]{0:T(128)}, u32[]{:S(2)}) copy-start(s32[32]{0:T(128)} %docs_ref.3) | copy-start | bytes 388
  2.1 7.2 %collective-permute-start.3 = (bf16[256,512]{1,0:T(8,128)(2,1)S(1)}, bf16[256,512]{1,0:T(8,128)(2,1)S(1)}, u32[]{:S(2)}, u32[]{:S(2)}) collective-permute-start(bf16[256,512]{1,0:T(8,128)(2,1)S(1)} %pad_maximum_fusion.6), channel_id=1, source_target_pairs={{0,1},{1,0},{2,3},{3,2},{4,5},{5,4},{6,7},{7,6},{8,9},{9,8},{10,11... | collective-permute-start | bytes 786440 | tf_op jit(solution)/shard_map/ppermute | solution.py:174
  2.4 12.8 %collective-permute-start = (bf16[256,512]{1,0:T(8,128)(2,1)S(1)}, bf16[256,512]{1,0:T(8,128)(2,1)S(1)}, u32[]{:S(2)}, u32[]{:S(2)}) collective-permute-start(bf16[256,512]{1,0:T(8,128)(2,1)S(1)} %pad_maximum_fusion.4), channel_id=1, source_target_pairs={{0,1},{1,0},{2,3},{3,2},{4,5},{5,4},{6,7},{7,6},{8,9},{9,8},{10,11... | collective-permute-start | bytes 786440 | tf_op jit(solution)/shard_map/ppermute | solution.py:174
  3.7 15.9 %collective-permute-start.2 = (bf16[256,512]{1,0:T(8,128)(2,1)S(1)}, bf16[256,512]{1,0:T(8,128)(2,1)S(1)}, u32[]{:S(2)}, u32[]{:S(2)}) collective-permute-start(bf16[256,512]{1,0:T(8,128)(2,1)S(1)} %pad_maximum_fusion.5.refs_2_.refs_6_), channel_id=1, source_target_pairs={{0,2},{2,4},{4,6},{6,8},{8,10},{10,12},{12,14},{14,16},{16,18},{18... | collective-permute-start | bytes 786440 | tf_op jit(solution)/shard_map/ppermute | solution.py:170
  9.3 10.3 %collective-permute-start.4 = (bf16[256,512]{1,0:T(8,128)(2,1)S(1)}, bf16[256,512]{1,0:T(8,128)(2,1)S(1)}, u32[]{:S(2)}, u32[]{:S(2)}) collective-permute-start(bf16[256,512]{1,0:T(8,128)(2,1)S(1)} %collective-permute-done.3.refs_3_.refs_7_), channel_id=1, source_target_pairs={{0,2},{2,4},{4,6},{6,8},{8,10},{10,12},{12,14},{14,16},{16,18},{18... | collective-permute-start | bytes 786440 | tf_op jit(solution)/shard_map/ppermute | solution.py:170
  15.2 22.7 %collective-permute-start.1 = (bf16[512,512]{1,0:T(8,128)(2,1)S(1)}, bf16[512,512]{1,0:T(8,128)(2,1)S(1)}, u32[]{:S(2)}, u32[]{:S(2)}) collective-permute-start(bf16[512,512]{1,0:T(8,128)(2,1)S(1)} %pad_maximum_fusion), channel_id=1, source_target_pairs={{0,2},{2,4},{4,6},{6,8},{8,10},{10,12},{12,14},{14,16},{16,18},{18... | collective-permute-start | bytes 1572872 | tf_op jit(solution)/shard_map/ppermute | solution.py:170
  35.8 29.5 %collective-permute-start.5 = (bf16[512,512]{1,0:T(8,128)(2,1)S(1)}, bf16[512,512]{1,0:T(8,128)(2,1)S(1)}, u32[]{:S(2)}, u32[]{:S(2)}) collective-permute-start(bf16[512,512]{1,0:T(8,128)(2,1)S(1)} %maximum_maximum_fusion), channel_id=1, source_target_pairs={{2,0},{4,2},{6,4},{8,6},{10,8},{12,10},{14,12},{16,14},{18,16},{20... | collective-permute-start | bytes 1572872 | tf_op jit(solution)/shard_map/ppermute | solution.py:170
  54.2 11.6 %collective-permute-start.8 = (bf16[256,512]{1,0:T(8,128)(2,1)S(1)}, bf16[256,512]{1,0:T(8,128)(2,1)S(1)}, u32[]{:S(2)}, u32[]{:S(2)}) collective-permute-start(bf16[256,512]{1,0:T(8,128)(2,1)S(1)} %pad_maximum_fusion.8), channel_id=1, source_target_pairs={{2,0},{4,2},{6,4},{8,6},{10,8},{12,10},{14,12},{16,14},{18,16},{20... | collective-permute-start | bytes 786440 | tf_op jit(solution)/shard_map/ppermute | solution.py:170
  57.5 9.6 %collective-permute-start.7 = (bf16[256,512]{1,0:T(8,128)(2,1)S(1)}, bf16[256,512]{1,0:T(8,128)(2,1)S(1)}, u32[]{:S(2)}, u32[]{:S(2)}) collective-permute-start(bf16[256,512]{1,0:T(8,128)(2,1)S(1)} %pad_maximum_fusion.7), channel_id=1, source_target_pairs={{2,0},{4,2},{6,4},{8,6},{10,8},{12,10},{14,12},{16,14},{18,16},{20... | collective-permute-start | bytes 786440 | tf_op jit(solution)/shard_map/ppermute | solution.py:170
  65.5 8.0 %collective-permute-start.6 = (bf16[256,512]{1,0:T(8,128)(2,1)S(1)}, bf16[256,512]{1,0:T(8,128)(2,1)S(1)}, u32[]{:S(2)}, u32[]{:S(2)}) collective-permute-start(bf16[256,512]{1,0:T(8,128)(2,1)S(1)} %get-tuple-element.48), channel_id=1, source_target_pairs={{0,1},{1,0},{2,3},{3,2},{4,5},{5,4},{6,7},{7,6},{8,9},{9,8},{10,11... | collective-permute-start | bytes 786440 | tf_op jit(solution)/shard_map/ppermute | solution.py:174
  65.8 13.3 %collective-permute-start.9 = (bf16[256,512]{1,0:T(8,128)(2,1)S(1)}, bf16[256,512]{1,0:T(8,128)(2,1)S(1)}, u32[]{:S(2)}, u32[]{:S(2)}) collective-permute-start(bf16[256,512]{1,0:T(8,128)(2,1)S(1)} %fusion.3), channel_id=1, source_target_pairs={{0,1},{1,0},{2,3},{3,2},{4,5},{5,4},{6,7},{7,6},{8,9},{9,8},{10,11... | collective-permute-start | bytes 786440 | tf_op jit(solution)/shard_map/ppermute | solution.py:174

commit v3 on v2

v3 whole, which is shorter than its diff:
```python
import functools
import math

import jax
import jax.numpy as jnp
from jax import lax
from jax.experimental import pallas as pl
from jax.experimental.pallas import tpu as pltpu
from jax.sharding import PartitionSpec as P

H = 64
KVH = 8
HD = 128
G = H // KVH
NEG = -1e30
ROW_TILE = 128
KEY_STEP = 128
BF16 = jnp.bfloat16
F32 = jnp.float32
NT = (((1,), (1,)), ((), ()))
NN = (((1,), (0,)), ((), ()))
TN = (((0,), (0,)), ((), ()))


def attn_kernel(info_ref, start_ref, q_ref, do_ref, *refs, tokens, pieces, aliased):
    count = 2 * pieces
    kv_in, refs = refs[:count], refs[count:]
    if aliased:
        refs = refs[1:]
    dq_ref, dkv_out, refs = refs[0], refs[1 : 1 + count], refs[1 + count :]
    k_win, v_win, dk_acc, dv_acc, bias = refs
    rt = ROW_TILE
    n_tiles = tokens // rt
    part = tokens // pieces
    width = kv_in[0].shape[1] // 2
    scale = math.log2(math.e) / math.sqrt(HD)
    factor = 1.0 / math.sqrt(HD)
    base = info_ref[0] * tokens
    first_off = pl.multiple_of(info_ref[1], part)
    if pieces == 1:
        places = [0, tokens]
    else:
        second_off = pl.multiple_of(part - first_off, part)
        places = [first_off, second_off, tokens + first_off, tokens + second_off]
    head = pl.program_id(0)
    k_cols = pl.ds(pl.multiple_of(head * HD, HD), HD)
    v_cols = pl.ds(pl.multiple_of(width + head * HD, HD), HD)

    @pl.when(head == 0)
    def _():
        for r in range(n_tiles):
            cols = slice(r * rt, (r + 1) * rt)
            pos = base + r * rt + lax.broadcasted_iota(jnp.int32, (1, rt), 1)
            key_pos = (
                base + r * rt - tokens + lax.broadcasted_iota(jnp.int32, (tokens + rt, rt), 0)
            )
            ok = (key_pos >= start_ref[:, cols]) & (key_pos <= pos)
            bias[r] = jnp.where(ok, 0.0, NEG).astype(F32)

    for place, kv in zip(places, kv_in):
        k_win[pl.ds(place, part), :] = kv[:, k_cols]
        v_win[pl.ds(place, part), :] = kv[:, v_cols]
    dk_acc[...] = jnp.zeros_like(dk_acc)
    dv_acc[...] = jnp.zeros_like(dv_acc)

    def row_tile(r, _):
        rows = pl.ds(pl.multiple_of(r * rt, rt), rt)
        for span in range(rt, tokens + rt + 1, KEY_STEP):

            @pl.when(info_ref[2 + r] == span)
            def _(span=span):
                over = tokens + rt - span
                window = pl.ds(pl.multiple_of(r * rt + over, KEY_STEP), span)
                k = k_win[window, :]
                v = v_win[window, :]
                mask = jnp.concatenate([bias[r, over:, :]] * G, axis=1)
                heads = [slice(h * HD, (h + 1) * HD) for h in range(G)]
                q = jnp.concatenate([q_ref[rows, s] for s in heads], axis=0)
                do = jnp.concatenate([do_ref[rows, s] for s in heads], axis=0)
                s = lax.dot_general(k, q, NT, preferred_element_type=F32) + mask
                dp = lax.dot_general(v, do, NT, preferred_element_type=F32)
                e = jnp.exp2((s - jnp.max(s, axis=0, keepdims=True)) * scale)
                inv = 1.0 / jnp.sum(e, axis=0, keepdims=True)
                delta = jnp.sum(e * dp, axis=0, keepdims=True) * inv
                p = e * inv
                ds = (p * (dp - delta)).astype(BF16)
                dv_acc[window, :] += lax.dot_general(
                    p.astype(BF16), do, NN, preferred_element_type=F32
                )
                dk_acc[window, :] += lax.dot_general(ds, q, NN, preferred_element_type=F32)
                dq = lax.dot_general(ds, k, TN, preferred_element_type=F32)
                dq = (dq * factor).astype(BF16)
                for h, s in enumerate(heads):
                    dq_ref[rows, s] = dq[h * rt : (h + 1) * rt]

        return 0

    lax.fori_loop(0, n_tiles, row_tile, 0)
    for place, dkv in zip(places, dkv_out):
        dkv[:, k_cols] = (dk_acc[pl.ds(place, part), :] * factor).astype(dkv.dtype)
        dkv[:, v_cols] = dv_acc[pl.ds(place, part), :].astype(dkv.dtype)


def attention(info, start, queries, grad_output, prev, own, grad_queries, chunk):
    tokens = queries.shape[0]
    pieces = len(own)
    part = tokens // pieces
    width = own[0].shape[1] // 2
    heads = width // HD
    first = chunk * heads
    wide = pl.BlockSpec((tokens, G * HD), lambda k: (0, first + k))
    whole = pl.BlockSpec((part, 2 * width), lambda k: (0, 0))
    scalars = pl.BlockSpec(memory_space=pltpu.SMEM)
    count = 2 * pieces
    aliased = grad_queries is not None
    work = 2 * tokens * G * HD * tokens * heads
    outs = pl.pallas_call(
        functools.partial(attn_kernel, tokens=tokens, pieces=pieces, aliased=aliased),
        grid=(heads,),
        in_specs=[scalars, pl.BlockSpec((1, tokens), lambda k: (0, 0)), wide, wide]
        + [whole] * count
        + ([pl.BlockSpec(memory_space=pl.ANY)] if aliased else []),
        out_specs=[wide] + [whole] * count,
        out_shape=[jax.ShapeDtypeStruct(queries.shape, BF16)]
        + [jax.ShapeDtypeStruct((part, 2 * width), BF16)] * pieces
        + [jax.ShapeDtypeStruct((part, 2 * width), F32)] * pieces,
        scratch_shapes=[pltpu.VMEM((2 * tokens, HD), BF16)] * 2
        + [pltpu.VMEM((2 * tokens, HD), F32)] * 2
        + [pltpu.VMEM((tokens // ROW_TILE, tokens + ROW_TILE, ROW_TILE), F32)],
        input_output_aliases={4 + count: 0} if aliased else {},
        compiler_params=pltpu.CompilerParams(vmem_limit_bytes=51 << 20),
        cost_estimate=pl.CostEstimate(
            flops=5 * work, bytes_accessed=3 * tokens * G * HD * 2 * heads, transcendentals=0
        ),
        name="attention",
    )(info, start, queries, grad_output, *prev, *own, *([grad_queries] if aliased else []))
    return outs[0], outs[1 : 1 + pieces], outs[1 + pieces :]


def documents(doc_lengths, shard, tokens, first_off):
    bounds = jnp.cumsum(doc_lengths)
    base = shard * tokens
    pos = base + jnp.arange(tokens, dtype=jnp.int32)
    start = jnp.max(jnp.where(pos[None, :] >= bounds[:, None], bounds[:, None], 0), axis=0)
    ends = base + ROW_TILE * (1 + jnp.arange(tokens // ROW_TILE, dtype=jnp.int32))
    spans = ends - start[::ROW_TILE] // KEY_STEP * KEY_STEP
    info = jnp.concatenate([jnp.stack([shard, first_off]), spans]).astype(jnp.int32)
    return info, start[None, :].astype(jnp.int32)


def shift(value, steps):
    count = lax.axis_size("ctx")
    first, last = max(0, -steps), min(count, count - steps)
    return lax.ppermute(value, "ctx", [(i, i + steps) for i in range(first, last)])


def swap(value):
    return lax.ppermute(value, "head", [(0, 1), (1, 0)])


def add(own, arrived):
    return (own + arrived.astype(F32)).astype(BF16)


def per_device(queries, key_rows, value_rows, grad_output, doc_lengths):
    tokens = queries.shape[0]
    head_count = lax.axis_size("head")
    kv_local = KVH // head_count
    local = kv_local * HD
    me = lax.axis_index("head")
    shard = lax.axis_index("ctx")
    chunks = 2 if kv_local % 2 == 0 else 1
    width = local // chunks
    cut = lambda x, start: lax.dynamic_slice_in_dim(x, start, width, axis=1)
    grad_queries = None

    if head_count == 2:
        half = tokens // 2
        info, start = documents(doc_lengths, shard, tokens, me * half)
        rows = (key_rows, value_rows)
        both = lambda at: jnp.concatenate([cut(x, at) for x in rows], axis=1)
        other = [both((1 - me) * local)]
        mine = [both(me * local + j * width) for j in range(chunks)]
        other += [both((1 - me) * local + j * width) for j in range(1, chunks)]
        recv = [swap(x) for x in other]
        prev = [[shift(mine[0], 1), shift(recv[0], 1)]]
        for j in range(1, chunks):
            arrived = shift(jnp.concatenate([mine[j], recv[j]], axis=0), 1)
            prev.append([arrived[:half], arrived[half:]])
        outs = [jnp.zeros_like(key_rows), jnp.zeros_like(value_rows)]
        earlier = None

        def put(part, at):
            for i in range(2):
                block = part[:, i * width : (i + 1) * width]
                outs[i] = lax.dynamic_update_slice_in_dim(outs[i], block, at, axis=1)

        for j in range(chunks):
            grad_queries, gone, own = attention(
                info, start, queries, grad_output, prev[j], [mine[j], recv[j]], grad_queries, j
            )
            if j < chunks - 1:
                back = shift(jnp.concatenate(gone, axis=0), -1)
                back = [back[:half], back[half:]]
                earlier = add(own[1], back[1])
            else:
                if earlier is not None:
                    put(swap(earlier), (1 - me) * local)
                back = shift(jnp.concatenate(gone, axis=0), -1)
                back = [back[:half], back[half:]]
                last = swap(add(own[1], back[1]))
            put(add(own[0], back[0]), me * local + j * width)
        put(last, (1 - me) * local + (chunks - 1) * width)
        return (grad_queries, *outs)

    info, start = documents(doc_lengths, shard, tokens, 0 * shard)
    key_own = lax.all_to_all(key_rows, "head", split_axis=1, concat_axis=0, tiled=True)
    val_own = lax.all_to_all(value_rows, "head", split_axis=1, concat_axis=0, tiled=True)
    totals = []
    for j in range(chunks):
        own = jnp.concatenate([cut(key_own, j * width), cut(val_own, j * width)], axis=1)
        grad_queries, gone, mine = attention(
            info, start, queries, grad_output, [shift(own, 1)], [own], grad_queries, j
        )
        totals.append(add(mine[0], shift(gone[0], -1)))
    outs = []
    for at in range(2):
        total = jnp.concatenate([x[:, at * width : (at + 1) * width] for x in totals], axis=1)
        outs.append(lax.all_to_all(total, "head", split_axis=0, concat_axis=1, tiled=True))
    return (grad_queries, *outs)


def solution(mesh):
    in_specs = (
        P("ctx", "head"),
        P(("ctx", "head"), None),
        P(("ctx", "head"), None),
        P("ctx", "head"),
        P(),
    )
    out_specs = (P("ctx", "head"), P(("ctx", "head"), None), P(("ctx", "head"), None))
    return jax.shard_map(
        per_device, mesh=mesh, in_specs=in_specs, out_specs=out_specs, check_vma=False
    )
```

time: 80.9 us -> 78 us (0.964)
  the two profiles are of different devices: /device:TPU:15 before, /device:TPU:12 now
where the time goes in v3:
time: 78 us; the launch traced here: 77.1 us
  Pallas kernels  37.4 us (48%)
  waiting for transfers between devices  22.1 us (28%)
  starting transfers between devices  12.4 us (16%)
  local copies, waits for them, and re-layouts  3.41 us (4%)
  other arithmetic  0.87 us (1%)
  between operations  0.85 us (1%)
    pallas_call x2, Pallas kernels, attention(): pl.pallas_call(functools.partial(attn_kernel, tokens=tokens, pieces=piece...  37.4 us
    ppermute x4, waiting for transfers between devices, swap(): return lax.ppermute(value, 'head', [(0, 1), (1, 0)])  13.9 us
    ppermute x5, starting transfers between devices, shift(): lax.ppermute(value, 'ctx', [(i, i + steps) for i in range(first, last)])  9.77 us
    ppermute x5, waiting for transfers between devices, shift(): lax.ppermute(value, 'ctx', [(i, i + steps) for i in range(first, last)])  8.21 us
    ppermute x4, starting transfers between devices, swap(): return lax.ppermute(value, 'head', [(0, 1), (1, 0)])  2.66 us
  transfers between devices with their start and end apart: 9, of which 6 were waited for; matrix products, arithmetic and copies ran while one was open for 2% of the time, Pallas kernels for 49%

profile of v3, /device:TPU:12, one launch (start us, length us, event | category | flops | bytes accessed | tf_op | source)
XLA Modules:
  0.0 77.1 jit_solution(404569500124486462)
XLA Ops:
  0.6 1.4 %constant_dynamic-slice_fusion = (bf16[256,256]{1,0:T(8,128)(2,1)S(1)}, bf16[256,256]{1,0:T(8,128)(2,1)S(1)}, bf16[256,256]{1,0:T(8,128)(2,1)S(1)}, bf16[256,256...) fusion(bf16[256,1024]{1,0:T(8,128)(2,1)} %param.7, ...), kind=kLoop, calls=%fused_computation.20 | loop fusion | bytes 2097168 | tf_op jit(solution)/shard_map/dynamic_slice | solution.py:174
  2.0 0.6 collective-permute-start.3
  2.6 1.9 %collective-permute-start.2 = (bf16[256,512]{1,0:T(8,128)(2,1)S(1)}, bf16[256,512]{1,0:T(8,128)(2,1)S(1)}, u32[]{:S(2)}, u32[]{:S(2)}) collective-permute-start(bf16[256,512]{1,0:T(8,128)(2,1)S(1)} %pad_maximum_fusion.5.refs_2_), channel_id=1, source_target_pairs={{0,2},{2,4},{4,6},{6,8},{8,10},{10,12},{12,14},{14,16},{16,18},{18... | collective-permute-start | bytes 786440 | tf_op jit(solution)/shard_map/ppermute | solution.py:154
  4.6 1.6 %collective-permute-start = (bf16[256,512]{1,0:T(8,128)(2,1)S(1)}, bf16[256,512]{1,0:T(8,128)(2,1)S(1)}, u32[]{:S(2)}, u32[]{:S(2)}) collective-permute-start(bf16[256,512]{1,0:T(8,128)(2,1)S(1)} %pad_maximum_fusion.4), channel_id=1, source_target_pairs={{0,1},{1,0},{2,3},{3,2},{4,5},{5,4},{6,7},{7,6},{8,9},{9,8},{10,11... | collective-permute-start | bytes 786440 | tf_op jit(solution)/shard_map/ppermute | solution.py:158
  6.2 0.7 copy.11
  6.9 0.1 reduce-window.8
  7.0 0.1 reduce
  7.1 0.1 select_reduce_fusion
  7.2 0.1 slice.45
  7.3 4.0 %collective-permute-done.3.refs_3_ = bf16[256,512]{1,0:T(8,128)(2,1)S(1)} collective-permute-done((bf16[256,512]{1,0:T(8,128)(2,1)S(1)}, bf16[256,512]{1,0:T(8,128)(2,1)S(1)}, u32[]{:S(2)}, u32[]{:S(2)}) %collective-permute-start.3) | collective-permute-done | bytes 262176 | tf_op jit(solution)/shard_map/ppermute | solution.py:158
  11.3 1.9 %collective-permute-start.4 = (bf16[256,512]{1,0:T(8,128)(2,1)S(1)}, bf16[256,512]{1,0:T(8,128)(2,1)S(1)}, u32[]{:S(2)}, u32[]{:S(2)}) collective-permute-start(bf16[256,512]{1,0:T(8,128)(2,1)S(1)} %collective-permute-done.3.refs_3_), channel_id=1, source_target_pairs={{0,2},{2,4},{4,6},{6,8},{8,10},{10,12},{12,14},{14,16},{16,18},{18... | collective-permute-start | bytes 786440 | tf_op jit(solution)/shard_map/ppermute | solution.py:154
  13.2 0.1 pad_add_fusion.info_ref
  13.3 2.5 %collective-permute-done.refs_3_ = bf16[256,512]{1,0:T(8,128)(2,1)S(1)} collective-permute-done((bf16[256,512]{1,0:T(8,128)(2,1)S(1)}, bf16[256,512]{1,0:T(8,128)(2,1)S(1)}, u32[]{:S(2)}, u32[]{:S(2)}) %collective-permute-start) | collective-permute-done | bytes 262176 | tf_op jit(solution)/shard_map/ppermute | solution.py:158
  15.8 1.9 %collective-permute-start.1 = (bf16[512,512]{1,0:T(8,128)(2,1)S(1)}, bf16[512,512]{1,0:T(8,128)(2,1)S(1)}, u32[]{:S(2)}, u32[]{:S(2)}) collective-permute-start(bf16[512,512]{1,0:T(8,128)(2,1)S(1)} %pad_maximum_fusion), channel_id=1, source_target_pairs={{0,2},{2,4},{4,6},{6,8},{8,10},{10,12},{12,14},{14,16},{16,18},{18... | collective-permute-start | bytes 1572872 | tf_op jit(solution)/shard_map/ppermute | solution.py:154
  17.7 0.0 collective-permute-done.2.refs_0_
  17.8 2.1 %collective-permute-done.4.refs_1_ = bf16[256,512]{1,0:T(8,128)(2,1)S(1)} collective-permute-done((bf16[256,512]{1,0:T(8,128)(2,1)S(1)}, bf16[256,512]{1,0:T(8,128)(2,1)S(1)}, u32[]{:S(2)}, u32[]{:S(2)}) %collective-permute-start.4) | collective-permute-done | bytes 262176 | tf_op jit(solution)/shard_map/ppermute | solution.py:154
  19.9 18.7 %attention.2 = (bf16[512,4096]{1,0:T(8,128)(2,1)}, bf16[256,512]{1,0:T(8,128)(2,1)S(1)}, bf16[256,512]{1,0:T(8,128)(2,1)S(1)}, f32[256,512]{1,0:T(8,128)S(1)}, f32[256,512]{1,0:T(8,128)S(1)}) custom-call(s32[6]{0:T(128)S(1)} %pad_add_fusion.info_ref, s32[1,512]{1,0:T(1,128)S(1)} %bitcast.4, bf16[512,4096]{1,0:T(8,128)(2,1)} %q_ref.3, ...), custom_call_target="tpu_custom_call" | custom-call | flops 5368709120 | bytes 6291456 | tf_op jit(solution)/shard_map/attention/pallas_call | solution.py:117
  38.6 2.1 %collective-permute-start.5 = (bf16[512,512]{1,0:T(8,128)(2,1)S(1)}, bf16[512,512]{1,0:T(8,128)(2,1)S(1)}, u32[]{:S(2)}, u32[]{:S(2)}) collective-permute-start(bf16[512,512]{1,0:T(8,128)(2,1)S(1)} %pad_maximum_fusion.1), channel_id=1, source_target_pairs={{2,0},{4,2},{6,4},{8,6},{10,8},{12,10},{14,12},{16,14},{18,16},{20... | collective-permute-start | bytes 1572872 | tf_op jit(solution)/shard_map/ppermute | solution.py:154
  40.8 0.0 collective-permute-done.1
  40.8 18.7 %attention.3 = (bf16[512,4096]{1,0:T(8,128)(2,1)}, bf16[256,512]{1,0:T(8,128)(2,1)S(1)}, bf16[256,512]{1,0:T(8,128)(2,1)S(1)}, f32[256,512]{1,0:T(8,128)S(1)}, f32[256,512]{1,0:T(8,128)S(1)}) custom-call(s32[6]{0:T(128)S(1)} %pad_add_fusion.info_ref, s32[1,512]{1,0:T(1,128)S(1)} %bitcast.5, ...), custom_call_target="tpu_custom_call", output_to_operand_aliasing={{0}: (8, {})} | custom-call | flops 5368709120 | bytes 6291456 | tf_op jit(solution)/shard_map/attention/pallas_call | solution.py:117
  59.6 1.9 %collective-permute-start.7 = (bf16[512,512]{1,0:T(8,128)(2,1)S(1)}, bf16[512,512]{1,0:T(8,128)(2,1)S(1)}, u32[]{:S(2)}, u32[]{:S(2)}) collective-permute-start(bf16[512,512]{1,0:T(8,128)(2,1)S(1)} %pad_maximum_fusion.2), channel_id=1, source_target_pairs={{2,0},{4,2},{6,4},{8,6},{10,8},{12,10},{14,12},{16,14},{18,16},{20... | collective-permute-start | bytes 1572872 | tf_op jit(solution)/shard_map/ppermute | solution.py:154
  61.5 0.0 collective-permute-done.5
  61.5 0.2 add_convert_fusion.2
  61.7 0.3 collective-permute-start.6
  61.9 0.1 broadcast.30.clone.1
  62.0 0.1 broadcast.30.clone
  62.1 6.1 %collective-permute-done.7 = bf16[512,512]{1,0:T(8,128)(2,1)S(1)} collective-permute-done((bf16[512,512]{1,0:T(8,128)(2,1)S(1)}, bf16[512,512]{1,0:T(8,128)(2,1)S(1)}, u32[]{:S(2)}, u32[]{:S(2)}) %collective-permute-start.7) | collective-permute-done | bytes 524320 | tf_op jit(solution)/shard_map/ppermute | solution.py:154
  68.2 0.2 add_convert_fusion
  68.3 0.3 collective-permute-start.8
  68.6 2.3 %collective-permute-done.6 = bf16[256,512]{1,0:T(8,128)(2,1)S(1)} collective-permute-done((bf16[256,512]{1,0:T(8,128)(2,1)S(1)}, bf16[256,512]{1,0:T(8,128)(2,1)S(1)}, u32[]{:S(2)}, u32[]{:S(2)}) %collective-permute-start.6) | collective-permute-done | bytes 262176 | tf_op jit(solution)/shard_map/ppermute | solution.py:158
  70.9 5.2 %collective-permute-done.8 = bf16[256,512]{1,0:T(8,128)(2,1)S(1)} collective-permute-done((bf16[256,512]{1,0:T(8,128)(2,1)S(1)}, bf16[256,512]{1,0:T(8,128)(2,1)S(1)}, u32[]{:S(2)}, u32[]{:S(2)}) %collective-permute-start.8) | collective-permute-done | bytes 262176 | tf_op jit(solution)/shard_map/ppermute | solution.py:158
  76.1 0.0 copy-start
  76.1 0.0 copy-start.1
  76.1 0.8 %copy-done = bf16[256,1024]{1,0:T(8,128)(2,1)} copy-done((bf16[256,1024]{1,0:T(8,128)(2,1)}, bf16[256,1024]{1,0:T(8,128)(2,1)S(1)}, u32[]{:S(2)}) %copy-start) | copy-done | bytes 524312
  76.9 0.2 copy-done.1
  (15 shorter events, 0.3 us)
Async XLA Ops:
  2.0 9.3 %collective-permute-start.3 = (bf16[256,512]{1,0:T(8,128)(2,1)S(1)}, bf16[256,512]{1,0:T(8,128)(2,1)S(1)}, u32[]{:S(2)}, u32[]{:S(2)}) collective-permute-start(bf16[256,512]{1,0:T(8,128)(2,1)S(1)} %pad_maximum_fusion.6), channel_id=1, source_target_pairs={{0,1},{1,0},{2,3},{3,2},{4,5},{5,4},{6,7},{7,6},{8,9},{9,8},{10,11... | collective-permute-start | bytes 786440 | tf_op jit(solution)/shard_map/ppermute | solution.py:158
  2.6 15.1 %collective-permute-start.2 = (bf16[256,512]{1,0:T(8,128)(2,1)S(1)}, bf16[256,512]{1,0:T(8,128)(2,1)S(1)}, u32[]{:S(2)}, u32[]{:S(2)}) collective-permute-start(bf16[256,512]{1,0:T(8,128)(2,1)S(1)} %pad_maximum_fusion.5.refs_2_), channel_id=1, source_target_pairs={{0,2},{2,4},{4,6},{6,8},{8,10},{10,12},{12,14},{14,16},{16,18},{18... | collective-permute-start | bytes 786440 | tf_op jit(solution)/shard_map/ppermute | solution.py:154
  4.6 11.2 %collective-permute-start = (bf16[256,512]{1,0:T(8,128)(2,1)S(1)}, bf16[256,512]{1,0:T(8,128)(2,1)S(1)}, u32[]{:S(2)}, u32[]{:S(2)}) collective-permute-start(bf16[256,512]{1,0:T(8,128)(2,1)S(1)} %pad_maximum_fusion.4), channel_id=1, source_target_pairs={{0,1},{1,0},{2,3},{3,2},{4,5},{5,4},{6,7},{7,6},{8,9},{9,8},{10,11... | collective-permute-start | bytes 786440 | tf_op jit(solution)/shard_map/ppermute | solution.py:158
  11.3 8.6 %collective-permute-start.4 = (bf16[256,512]{1,0:T(8,128)(2,1)S(1)}, bf16[256,512]{1,0:T(8,128)(2,1)S(1)}, u32[]{:S(2)}, u32[]{:S(2)}) collective-permute-start(bf16[256,512]{1,0:T(8,128)(2,1)S(1)} %collective-permute-done.3.refs_3_), channel_id=1, source_target_pairs={{0,2},{2,4},{4,6},{6,8},{8,10},{10,12},{12,14},{14,16},{16,18},{18... | collective-permute-start | bytes 786440 | tf_op jit(solution)/shard_map/ppermute | solution.py:154
  15.8 24.9 %collective-permute-start.1 = (bf16[512,512]{1,0:T(8,128)(2,1)S(1)}, bf16[512,512]{1,0:T(8,128)(2,1)S(1)}, u32[]{:S(2)}, u32[]{:S(2)}) collective-permute-start(bf16[512,512]{1,0:T(8,128)(2,1)S(1)} %pad_maximum_fusion), channel_id=1, source_target_pairs={{0,2},{2,4},{4,6},{6,8},{8,10},{10,12},{12,14},{14,16},{16,18},{18... | collective-permute-start | bytes 1572872 | tf_op jit(solution)/shard_map/ppermute | solution.py:154
  38.6 22.9 %collective-permute-start.5 = (bf16[512,512]{1,0:T(8,128)(2,1)S(1)}, bf16[512,512]{1,0:T(8,128)(2,1)S(1)}, u32[]{:S(2)}, u32[]{:S(2)}) collective-permute-start(bf16[512,512]{1,0:T(8,128)(2,1)S(1)} %pad_maximum_fusion.1), channel_id=1, source_target_pairs={{2,0},{4,2},{6,4},{8,6},{10,8},{12,10},{14,12},{16,14},{18,16},{20... | collective-permute-start | bytes 1572872 | tf_op jit(solution)/shard_map/ppermute | solution.py:154
  59.6 8.6 %collective-permute-start.7 = (bf16[512,512]{1,0:T(8,128)(2,1)S(1)}, bf16[512,512]{1,0:T(8,128)(2,1)S(1)}, u32[]{:S(2)}, u32[]{:S(2)}) collective-permute-start(bf16[512,512]{1,0:T(8,128)(2,1)S(1)} %pad_maximum_fusion.2), channel_id=1, source_target_pairs={{2,0},{4,2},{6,4},{8,6},{10,8},{12,10},{14,12},{16,14},{18,16},{20... | collective-permute-start | bytes 1572872 | tf_op jit(solution)/shard_map/ppermute | solution.py:154
  61.7 9.2 %collective-permute-start.6 = (bf16[256,512]{1,0:T(8,128)(2,1)S(1)}, bf16[256,512]{1,0:T(8,128)(2,1)S(1)}, u32[]{:S(2)}, u32[]{:S(2)}) collective-permute-start(bf16[256,512]{1,0:T(8,128)(2,1)S(1)} %get-tuple-element.25), channel_id=1, source_target_pairs={{0,1},{1,0},{2,3},{3,2},{4,5},{5,4},{6,7},{7,6},{8,9},{9,8},{10,11... | collective-permute-start | bytes 786440 | tf_op jit(solution)/shard_map/ppermute | solution.py:158
  68.3 7.7 %collective-permute-start.8 = (bf16[256,512]{1,0:T(8,128)(2,1)S(1)}, bf16[256,512]{1,0:T(8,128)(2,1)S(1)}, u32[]{:S(2)}, u32[]{:S(2)}) collective-permute-start(bf16[256,512]{1,0:T(8,128)(2,1)S(1)} %get-tuple-element.23), channel_id=1, source_target_pairs={{0,1},{1,0},{2,3},{3,2},{4,5},{5,4},{6,7},{7,6},{8,9},{9,8},{10,11... | collective-permute-start | bytes 786440 | tf_op jit(solution)/shard_map/ppermute | solution.py:158
  76.1 0.8 %copy-start = (bf16[256,1024]{1,0:T(8,128)(2,1)}, bf16[256,1024]{1,0:T(8,128)(2,1)S(1)}, u32[]{:S(2)}) copy-start(bf16[256,1024]{1,0:T(8,128)(2,1)S(1)} %get-tuple-element.37) | copy-start | bytes 1572868
  76.1 1.0 %copy-start.1 = (bf16[256,1024]{1,0:T(8,128)(2,1)}, bf16[256,1024]{1,0:T(8,128)(2,1)S(1)}, u32[]{:S(2)}) copy-start(bf16[256,1024]{1,0:T(8,128)(2,1)S(1)} %get-tuple-element.38) | copy-start | bytes 1572868

commit v4 on v3

--- a/solution.py
+++ b/solution.py
@@ -22,13 +22,13 @@
 TN = (((0,), (0,)), ((), ()))
 
 
-def attn_kernel(info_ref, start_ref, q_ref, do_ref, *refs, tokens, pieces, aliased):
+def attn_kernel(info_ref, start_ref, q_ref, do_ref, *refs, tokens, pieces, aliased, first):
     count = 2 * pieces
     kv_in, refs = refs[:count], refs[count:]
     if aliased:
         refs = refs[1:]
     dq_ref, dkv_out, refs = refs[0], refs[1 : 1 + count], refs[1 + count :]
-    k_win, v_win, dk_acc, dv_acc, bias = refs
+    k_win, v_win, dk_acc, dv_acc, bias, q_buf, do_buf, dq_buf, sems = refs
     rt = ROW_TILE
     n_tiles = tokens // rt
     part = tokens // pieces
@@ -46,8 +46,24 @@
     k_cols = pl.ds(pl.multiple_of(head * HD, HD), HD)
     v_cols = pl.ds(pl.multiple_of(width + head * HD, HD), HD)
 
+    heads_here = width // HD
+
+    def copies(h, r):
+        rows = pl.ds(r * rt, rt)
+        cols = pl.ds(pl.multiple_of((first + h) * G * HD, G * HD), G * HD)
+        return (
+            pltpu.make_async_copy(q_ref.at[rows, cols], q_buf.at[h, rows, :], sems.at[0, h, r]),
+            pltpu.make_async_copy(do_ref.at[rows, cols], do_buf.at[h, rows, :], sems.at[1, h, r]),
+            pltpu.make_async_copy(dq_buf.at[h, rows, :], dq_ref.at[rows, cols], sems.at[2, h, r]),
+        )
+
     @pl.when(head == 0)
     def _():
+        for h in range(heads_here):
+            for r in range(n_tiles):
+                get_q, get_do, _ = copies(h, r)
+                get_q.start()
+                get_do.start()
         for r in range(n_tiles):
             cols = slice(r * rt, (r + 1) * rt)
             pos = base + r * rt + lax.broadcasted_iota(jnp.int32, (1, rt), 1)
@@ -65,6 +81,9 @@
 
     def row_tile(r, _):
         rows = pl.ds(pl.multiple_of(r * rt, rt), rt)
+        get_q, get_do, put_dq = copies(head, r)
+        get_q.wait()
+        get_do.wait()
         for span in range(rt, tokens + rt + 1, KEY_STEP):
 
             @pl.when(info_ref[2 + r] == span)
@@ -75,8 +94,8 @@
                 v = v_win[window, :]
                 mask = jnp.concatenate([bias[r, over:, :]] * G, axis=1)
                 heads = [slice(h * HD, (h + 1) * HD) for h in range(G)]
-                q = jnp.concatenate([q_ref[rows, s] for s in heads], axis=0)
-                do = jnp.concatenate([do_ref[rows, s] for s in heads], axis=0)
+                q = jnp.concatenate([q_buf[head, rows, s] for s in heads], axis=0)
+                do = jnp.concatenate([do_buf[head, rows, s] for s in heads], axis=0)
                 s = lax.dot_general(k, q, NT, preferred_element_type=F32) + mask
                 dp = lax.dot_general(v, do, NT, preferred_element_type=F32)
                 e = jnp.exp2((s - jnp.max(s, axis=0, keepdims=True)) * scale)
@@ -91,14 +110,21 @@
                 dq = lax.dot_general(ds, k, TN, preferred_element_type=F32)
                 dq = (dq * factor).astype(BF16)
                 for h, s in enumerate(heads):
-                    dq_ref[rows, s] = dq[h * rt : (h + 1) * rt]
-
+                    dq_buf[head, rows, s] = dq[h * rt : (h + 1) * rt]
+
+        put_dq.start()
         return 0
 
     lax.fori_loop(0, n_tiles, row_tile, 0)
     for place, dkv in zip(places, dkv_out):
         dkv[:, k_cols] = (dk_acc[pl.ds(place, part), :] * factor).astype(dkv.dtype)
         dkv[:, v_cols] = dv_acc[pl.ds(place, part), :].astype(dkv.dtype)
+
+    @pl.when(head == heads_here - 1)
+    def _():
+        for h in range(heads_here):
+            for r in range(n_tiles):
+                copies(h, r)[2].wait()
 
 
 def attention(info, start, queries, grad_output, prev, own, grad_queries, chunk):
@@ -108,25 +134,28 @@
     width = own[0].shape[1] // 2
     heads = width // HD
     first = chunk * heads
-    wide = pl.BlockSpec((tokens, G * HD), lambda k: (0, first + k))
+    n_tiles = tokens // ROW_TILE
+    wide = pl.BlockSpec(memory_space=pltpu.HBM)
     whole = pl.BlockSpec((part, 2 * width), lambda k: (0, 0))
     scalars = pl.BlockSpec(memory_space=pltpu.SMEM)
     count = 2 * pieces
     aliased = grad_queries is not None
     work = 2 * tokens * G * HD * tokens * heads
     outs = pl.pallas_call(
-        functools.partial(attn_kernel, tokens=tokens, pieces=pieces, aliased=aliased),
+        functools.partial(attn_kernel, tokens=tokens, pieces=pieces, aliased=aliased, first=first),
         grid=(heads,),
         in_specs=[scalars, pl.BlockSpec((1, tokens), lambda k: (0, 0)), wide, wide]
         + [whole] * count
-        + ([pl.BlockSpec(memory_space=pl.ANY)] if aliased else []),
+        + ([wide] if aliased else []),
         out_specs=[wide] + [whole] * count,
         out_shape=[jax.ShapeDtypeStruct(queries.shape, BF16)]
         + [jax.ShapeDtypeStruct((part, 2 * width), BF16)] * pieces
         + [jax.ShapeDtypeStruct((part, 2 * width), F32)] * pieces,
         scratch_shapes=[pltpu.VMEM((2 * tokens, HD), BF16)] * 2
         + [pltpu.VMEM((2 * tokens, HD), F32)] * 2
-        + [pltpu.VMEM((tokens // ROW_TILE, tokens + ROW_TILE, ROW_TILE), F32)],
+        + [pltpu.VMEM((n_tiles, tokens + ROW_TILE, ROW_TILE), F32)]
+        + [pltpu.VMEM((heads, tokens, G * HD), BF16)] * 3
+        + [pltpu.SemaphoreType.DMA((3, heads, n_tiles))],
         input_output_aliases={4 + count: 0} if aliased else {},
         compiler_params=pltpu.CompilerParams(vmem_limit_bytes=51 << 20),
         cost_estimate=pl.CostEstimate(

time: 78 us -> 77.6 us (level)
  the two profiles are of different devices: /device:TPU:12 before, /device:TPU:15 now
where the time goes in v4:
time: 77.6 us; the launch traced here: 76.6 us
  Pallas kernels  32.4 us (42%)
  starting transfers between devices  23.9 us (31%)
  waiting for transfers between devices  15.1 us (19%)
  local copies, waits for them, and re-layouts  3.41 us (4%)
  between operations  0.91 us (1%)
  other arithmetic  0.87 us (1%)
    pallas_call x2, Pallas kernels, attention(): pl.pallas_call(functools.partial(attn_kernel, tokens=tokens, pieces=piece...  32.4 us
    ppermute x5, starting transfers between devices, shift(): lax.ppermute(value, 'ctx', [(i, i + steps) for i in range(first, last)])  22.1 us
    ppermute x4, waiting for transfers between devices, swap(): return lax.ppermute(value, 'head', [(0, 1), (1, 0)])  8.07 us
    ppermute x5, waiting for transfers between devices, shift(): lax.ppermute(value, 'ctx', [(i, i + steps) for i in range(first, last)])  7.06 us
    ppermute x4, starting transfers between devices, swap(): return lax.ppermute(value, 'head', [(0, 1), (1, 0)])  1.74 us
  transfers between devices with their start and end apart: 9, of which 4 were waited for; matrix products, arithmetic and copies ran while one was open for 2% of the time, Pallas kernels for 42%

profile of v4, /device:TPU:15, one launch (start us, length us, event | category | flops | bytes accessed | tf_op | source)
XLA Modules:
  0.0 76.6 jit_solution(16619880801118216656)
XLA Ops:
  0.6 1.4 %constant_dynamic-slice_fusion = (bf16[256,256]{1,0:T(8,128)(2,1)S(1)}, bf16[256,256]{1,0:T(8,128)(2,1)S(1)}, bf16[256,256]{1,0:T(8,128)(2,1)S(1)}, bf16[256,256...) fusion(bf16[256,1024]{1,0:T(8,128)(2,1)} %param.7, ...), kind=kLoop, calls=%fused_computation.20 | loop fusion | bytes 2097168 | tf_op jit(solution)/shard_map/dynamic_slice | solution.py:203
  2.0 0.3 collective-permute-start.3
  2.4 4.0 %collective-permute-start.2 = (bf16[256,512]{1,0:T(8,128)(2,1)S(1)}, bf16[256,512]{1,0:T(8,128)(2,1)S(1)}, u32[]{:S(2)}, u32[]{:S(2)}) collective-permute-start(bf16[256,512]{1,0:T(8,128)(2,1)S(1)} %pad_maximum_fusion.5.refs_2_), channel_id=1, source_target_pairs={{0,2},{2,4},{4,6},{6,8},{8,10},{10,12},{12,14},{14,16},{16,18},{18... | collective-permute-start | bytes 786440 | tf_op jit(solution)/shard_map/ppermute | solution.py:183
  6.4 1.3 %collective-permute-start = (bf16[256,512]{1,0:T(8,128)(2,1)S(1)}, bf16[256,512]{1,0:T(8,128)(2,1)S(1)}, u32[]{:S(2)}, u32[]{:S(2)}) collective-permute-start(bf16[256,512]{1,0:T(8,128)(2,1)S(1)} %pad_maximum_fusion.4), channel_id=1, source_target_pairs={{0,1},{1,0},{2,3},{3,2},{4,5},{5,4},{6,7},{7,6},{8,9},{9,8},{10,11... | collective-permute-start | bytes 786440 | tf_op jit(solution)/shard_map/ppermute | solution.py:187
  7.7 0.7 copy.11
  8.5 0.1 reduce-window.8
  8.5 0.1 reduce
  8.6 0.1 select_reduce_fusion
  8.7 0.1 slice.45
  8.8 0.4 collective-permute-done.3.refs_3_
  9.3 5.7 %collective-permute-start.4 = (bf16[256,512]{1,0:T(8,128)(2,1)S(1)}, bf16[256,512]{1,0:T(8,128)(2,1)S(1)}, u32[]{:S(2)}, u32[]{:S(2)}) collective-permute-start(bf16[256,512]{1,0:T(8,128)(2,1)S(1)} %collective-permute-done.3.refs_3_), channel_id=1, source_target_pairs={{0,2},{2,4},{4,6},{6,8},{8,10},{10,12},{12,14},{14,16},{16,18},{18... | collective-permute-start | bytes 786440 | tf_op jit(solution)/shard_map/ppermute | solution.py:183
  15.0 0.1 pad_add_fusion.info_ref
  15.1 0.0 collective-permute-done.refs_3_
  15.2 4.4 %collective-permute-start.1 = (bf16[512,512]{1,0:T(8,128)(2,1)S(1)}, bf16[512,512]{1,0:T(8,128)(2,1)S(1)}, u32[]{:S(2)}, u32[]{:S(2)}) collective-permute-start(bf16[512,512]{1,0:T(8,128)(2,1)S(1)} %pad_maximum_fusion), channel_id=1, source_target_pairs={{0,2},{2,4},{4,6},{6,8},{8,10},{10,12},{12,14},{14,16},{16,18},{18... | collective-permute-start | bytes 1572872 | tf_op jit(solution)/shard_map/ppermute | solution.py:183
  19.6 0.0 collective-permute-done.2.refs_0_
  19.6 0.0 collective-permute-done.4.refs_1_
  19.6 16.2 %attention.2 = (bf16[512,4096]{1,0:T(8,128)(2,1)}, bf16[256,512]{1,0:T(8,128)(2,1)S(1)}, bf16[256,512]{1,0:T(8,128)(2,1)S(1)}, f32[256,512]{1,0:T(8,128)S(1)}, f32[256,512]{1,0:T(8,128)S(1)}) custom-call(s32[6]{0:T(128)S(1)} %pad_add_fusion.info_ref, s32[1,512]{1,0:T(1,128)S(1)} %bitcast.4, bf16[512,4096]{1,0:T(8,128)(2,1)} %q_ref.3, ...), custom_call_target="tpu_custom_call" | custom-call | flops 5368709120 | bytes 6291456 | tf_op jit(solution)/shard_map/attention/pallas_call | solution.py:144
  35.9 4.1 %collective-permute-start.5 = (bf16[512,512]{1,0:T(8,128)(2,1)S(1)}, bf16[512,512]{1,0:T(8,128)(2,1)S(1)}, u32[]{:S(2)}, u32[]{:S(2)}) collective-permute-start(bf16[512,512]{1,0:T(8,128)(2,1)S(1)} %pad_maximum_fusion.1), channel_id=1, source_target_pairs={{2,0},{4,2},{6,4},{8,6},{10,8},{12,10},{14,12},{16,14},{18,16},{20... | collective-permute-start | bytes 1572872 | tf_op jit(solution)/shard_map/ppermute | solution.py:183
  40.0 0.0 collective-permute-done.1
  40.0 16.2 %attention.3 = (bf16[512,4096]{1,0:T(8,128)(2,1)}, bf16[256,512]{1,0:T(8,128)(2,1)S(1)}, bf16[256,512]{1,0:T(8,128)(2,1)S(1)}, f32[256,512]{1,0:T(8,128)S(1)}, f32[256,512]{1,0:T(8,128)S(1)}) custom-call(s32[6]{0:T(128)S(1)} %pad_add_fusion.info_ref, s32[1,512]{1,0:T(1,128)S(1)} %bitcast.5, ...), custom_call_target="tpu_custom_call", output_to_operand_aliasing={{0}: (8, {})} | custom-call | flops 5368709120 | bytes 6291456 | tf_op jit(solution)/shard_map/attention/pallas_call | solution.py:144
  56.3 3.9 %collective-permute-start.7 = (bf16[512,512]{1,0:T(8,128)(2,1)S(1)}, bf16[512,512]{1,0:T(8,128)(2,1)S(1)}, u32[]{:S(2)}, u32[]{:S(2)}) collective-permute-start(bf16[512,512]{1,0:T(8,128)(2,1)S(1)} %pad_maximum_fusion.2), channel_id=1, source_target_pairs={{2,0},{4,2},{6,4},{8,6},{10,8},{12,10},{14,12},{16,14},{18,16},{20... | collective-permute-start | bytes 1572872 | tf_op jit(solution)/shard_map/ppermute | solution.py:183
  60.2 0.0 collective-permute-done.5
  60.2 0.2 add_convert_fusion.2
  60.4 0.1 collective-permute-start.6
  60.4 0.1 broadcast.30.clone.1
  60.5 0.1 broadcast.30.clone
  60.6 7.0 %collective-permute-done.7 = bf16[512,512]{1,0:T(8,128)(2,1)S(1)} collective-permute-done((bf16[512,512]{1,0:T(8,128)(2,1)S(1)}, bf16[512,512]{1,0:T(8,128)(2,1)S(1)}, u32[]{:S(2)}, u32[]{:S(2)}) %collective-permute-start.7) | collective-permute-done | bytes 524320 | tf_op jit(solution)/shard_map/ppermute | solution.py:183
  67.7 0.2 add_convert_fusion
  67.8 0.1 collective-permute-start.8
  67.9 0.4 collective-permute-done.6
  68.4 7.2 %collective-permute-done.8 = bf16[256,512]{1,0:T(8,128)(2,1)S(1)} collective-permute-done((bf16[256,512]{1,0:T(8,128)(2,1)S(1)}, bf16[256,512]{1,0:T(8,128)(2,1)S(1)}, u32[]{:S(2)}, u32[]{:S(2)}) %collective-permute-start.8) | collective-permute-done | bytes 262176 | tf_op jit(solution)/shard_map/ppermute | solution.py:187
  75.6 0.0 copy-start
  75.6 0.0 copy-start.1
  75.7 0.8 %copy-done = bf16[256,1024]{1,0:T(8,128)(2,1)} copy-done((bf16[256,1024]{1,0:T(8,128)(2,1)}, bf16[256,1024]{1,0:T(8,128)(2,1)S(1)}, u32[]{:S(2)}) %copy-start) | copy-done | bytes 524312
  76.4 0.2 copy-done.1
  (15 shorter events, 0.3 us)
Async XLA Ops:
  2.0 7.2 %collective-permute-start.3 = (bf16[256,512]{1,0:T(8,128)(2,1)S(1)}, bf16[256,512]{1,0:T(8,128)(2,1)S(1)}, u32[]{:S(2)}, u32[]{:S(2)}) collective-permute-start(bf16[256,512]{1,0:T(8,128)(2,1)S(1)} %pad_maximum_fusion.6), channel_id=1, source_target_pairs={{0,1},{1,0},{2,3},{3,2},{4,5},{5,4},{6,7},{7,6},{8,9},{9,8},{10,11... | collective-permute-start | bytes 786440 | tf_op jit(solution)/shard_map/ppermute | solution.py:187
  2.4 17.2 %collective-permute-start.2 = (bf16[256,512]{1,0:T(8,128)(2,1)S(1)}, bf16[256,512]{1,0:T(8,128)(2,1)S(1)}, u32[]{:S(2)}, u32[]{:S(2)}) collective-permute-start(bf16[256,512]{1,0:T(8,128)(2,1)S(1)} %pad_maximum_fusion.5.refs_2_), channel_id=1, source_target_pairs={{0,2},{2,4},{4,6},{6,8},{8,10},{10,12},{12,14},{14,16},{16,18},{18... | collective-permute-start | bytes 786440 | tf_op jit(solution)/shard_map/ppermute | solution.py:183
  6.4 8.7 %collective-permute-start = (bf16[256,512]{1,0:T(8,128)(2,1)S(1)}, bf16[256,512]{1,0:T(8,128)(2,1)S(1)}, u32[]{:S(2)}, u32[]{:S(2)}) collective-permute-start(bf16[256,512]{1,0:T(8,128)(2,1)S(1)} %pad_maximum_fusion.4), channel_id=1, source_target_pairs={{0,1},{1,0},{2,3},{3,2},{4,5},{5,4},{6,7},{7,6},{8,9},{9,8},{10,11... | collective-permute-start | bytes 786440 | tf_op jit(solution)/shard_map/ppermute | solution.py:187
  9.3 10.3 %collective-permute-start.4 = (bf16[256,512]{1,0:T(8,128)(2,1)S(1)}, bf16[256,512]{1,0:T(8,128)(2,1)S(1)}, u32[]{:S(2)}, u32[]{:S(2)}) collective-permute-start(bf16[256,512]{1,0:T(8,128)(2,1)S(1)} %collective-permute-done.3.refs_3_), channel_id=1, source_target_pairs={{0,2},{2,4},{4,6},{6,8},{8,10},{10,12},{12,14},{14,16},{16,18},{18... | collective-permute-start | bytes 786440 | tf_op jit(solution)/shard_map/ppermute | solution.py:183
  15.2 24.8 %collective-permute-start.1 = (bf16[512,512]{1,0:T(8,128)(2,1)S(1)}, bf16[512,512]{1,0:T(8,128)(2,1)S(1)}, u32[]{:S(2)}, u32[]{:S(2)}) collective-permute-start(bf16[512,512]{1,0:T(8,128)(2,1)S(1)} %pad_maximum_fusion), channel_id=1, source_target_pairs={{0,2},{2,4},{4,6},{6,8},{8,10},{10,12},{12,14},{14,16},{16,18},{18... | collective-permute-start | bytes 1572872 | tf_op jit(solution)/shard_map/ppermute | solution.py:183
  35.9 24.3 %collective-permute-start.5 = (bf16[512,512]{1,0:T(8,128)(2,1)S(1)}, bf16[512,512]{1,0:T(8,128)(2,1)S(1)}, u32[]{:S(2)}, u32[]{:S(2)}) collective-permute-start(bf16[512,512]{1,0:T(8,128)(2,1)S(1)} %pad_maximum_fusion.1), channel_id=1, source_target_pairs={{2,0},{4,2},{6,4},{8,6},{10,8},{12,10},{14,12},{16,14},{18,16},{20... | collective-permute-start | bytes 1572872 | tf_op jit(solution)/shard_map/ppermute | solution.py:183
  56.3 11.4 %collective-permute-start.7 = (bf16[512,512]{1,0:T(8,128)(2,1)S(1)}, bf16[512,512]{1,0:T(8,128)(2,1)S(1)}, u32[]{:S(2)}, u32[]{:S(2)}) collective-permute-start(bf16[512,512]{1,0:T(8,128)(2,1)S(1)} %pad_maximum_fusion.2), channel_id=1, source_target_pairs={{2,0},{4,2},{6,4},{8,6},{10,8},{12,10},{14,12},{16,14},{18,16},{20... | collective-permute-start | bytes 1572872 | tf_op jit(solution)/shard_map/ppermute | solution.py:183
  60.4 8.0 %collective-permute-start.6 = (bf16[256,512]{1,0:T(8,128)(2,1)S(1)}, bf16[256,512]{1,0:T(8,128)(2,1)S(1)}, u32[]{:S(2)}, u32[]{:S(2)}) collective-permute-start(bf16[256,512]{1,0:T(8,128)(2,1)S(1)} %get-tuple-element.25), channel_id=1, source_target_pairs={{0,1},{1,0},{2,3},{3,2},{4,5},{5,4},{6,7},{7,6},{8,9},{9,8},{10,11... | collective-permute-start | bytes 786440 | tf_op jit(solution)/shard_map/ppermute | solution.py:187
  67.8 7.8 %collective-permute-start.8 = (bf16[256,512]{1,0:T(8,128)(2,1)S(1)}, bf16[256,512]{1,0:T(8,128)(2,1)S(1)}, u32[]{:S(2)}, u32[]{:S(2)}) collective-permute-start(bf16[256,512]{1,0:T(8,128)(2,1)S(1)} %get-tuple-element.23), channel_id=1, source_target_pairs={{0,1},{1,0},{2,3},{3,2},{4,5},{5,4},{6,7},{7,6},{8,9},{9,8},{10,11... | collective-permute-start | bytes 786440 | tf_op jit(solution)/shard_map/ppermute | solution.py:187
  75.6 0.8 %copy-start = (bf16[256,1024]{1,0:T(8,128)(2,1)}, bf16[256,1024]{1,0:T(8,128)(2,1)S(1)}, u32[]{:S(2)}) copy-start(bf16[256,1024]{1,0:T(8,128)(2,1)S(1)} %get-tuple-element.37) | copy-start | bytes 1572868
  75.6 1.0 %copy-start.1 = (bf16[256,1024]{1,0:T(8,128)(2,1)}, bf16[256,1024]{1,0:T(8,128)(2,1)S(1)}, u32[]{:S(2)}) copy-start(bf16[256,1024]{1,0:T(8,128)(2,1)S(1)} %get-tuple-element.38) | copy-start | bytes 1572868

commit v5 on v4

--- a/solution.py
+++ b/solution.py
@@ -14,7 +14,7 @@
 G = H // KVH
 NEG = -1e30
 ROW_TILE = 128
-KEY_STEP = 128
+KEY_STEP = 64
 BF16 = jnp.bfloat16
 F32 = jnp.float32
 NT = (((1,), (1,)), ((), ()))

time: 77.6 us -> 76.4 us (0.985); the launches traced: 76.6 us -> 76.6 us
  Pallas kernels: 32.4 us -> 37.1 us
  starting transfers between devices: 23.9 us -> 20.1 us
  waiting for transfers between devices: 15.1 us -> 14.2 us
    pallas_call x2, Pallas kernels: 32.4 us -> 37.1 us  [attention(): pl.pallas_call(functools.partial(attn_kernel, tokens=tokens, pieces=piece...]
    ppermute x5, starting transfers between devices: 22.1 us -> 18 us  [shift(): lax.ppermute(value, 'ctx', [(i, i + steps) for i in range(first, last)])]
    ppermute x4, waiting for transfers between devices: 8.07 us -> 5.39 us  [swap(): return lax.ppermute(value, 'head', [(0, 1), (1, 0)])]
    ppermute x5, waiting for transfers between devices: 7.06 us -> 8.86 us  [shift(): lax.ppermute(value, 'ctx', [(i, i + steps) for i in range(first, last)])]
  transfers between devices with their start and end apart: 9 -> 9, of which waited for: 4 -> 3; matrix products, arithmetic and copies ran while one was open for 2% -> 2% of each run, Pallas kernels for 42% -> 48%
where the time goes in v5:
time: 76.4 us; the launch traced here: 76.6 us
  Pallas kernels  37.1 us (49%)
  starting transfers between devices  20.1 us (26%)
  waiting for transfers between devices  14.2 us (19%)
  local copies, waits for them, and re-layouts  3.41 us (4%)
  between operations  0.89 us (1%)
  other arithmetic  0.87 us (1%)
    pallas_call x2, Pallas kernels, attention(): pl.pallas_call(functools.partial(attn_kernel, tokens=tokens, pieces=piece...  37.1 us
    ppermute x5, starting transfers between devices, shift(): lax.ppermute(value, 'ctx', [(i, i + steps) for i in range(first, last)])  18 us
    ppermute x5, waiting for transfers between devices, shift(): lax.ppermute(value, 'ctx', [(i, i + steps) for i in range(first, last)])  8.86 us
    ppermute x4, waiting for transfers between devices, swap(): return lax.ppermute(value, 'head', [(0, 1), (1, 0)])  5.39 us
    ppermute x4, starting transfers between devices, swap(): return lax.ppermute(value, 'head', [(0, 1), (1, 0)])  2.15 us
  transfers between devices with their start and end apart: 9, of which 3 were waited for; matrix products, arithmetic and copies ran while one was open for 2% of the time, Pallas kernels for 48%

profile of v5, /device:TPU:15, one launch (start us, length us, event | category | flops | bytes accessed | tf_op | source)
XLA Modules:
  0.0 76.6 jit_solution(8336827827614674908)
XLA Ops:
  0.6 1.4 %constant_dynamic-slice_fusion = (bf16[256,256]{1,0:T(8,128)(2,1)S(1)}, bf16[256,256]{1,0:T(8,128)(2,1)S(1)}, bf16[256,256]{1,0:T(8,128)(2,1)S(1)}, bf16[256,256...) fusion(bf16[256,1024]{1,0:T(8,128)(2,1)} %param.7, ...), kind=kLoop, calls=%fused_computation.20 | loop fusion | bytes 2097168 | tf_op jit(solution)/shard_map/dynamic_slice | solution.py:203
  2.0 0.3 collective-permute-start.3
  2.4 4.0 %collective-permute-start.2 = (bf16[256,512]{1,0:T(8,128)(2,1)S(1)}, bf16[256,512]{1,0:T(8,128)(2,1)S(1)}, u32[]{:S(2)}, u32[]{:S(2)}) collective-permute-start(bf16[256,512]{1,0:T(8,128)(2,1)S(1)} %pad_maximum_fusion.5.refs_2_), channel_id=1, source_target_pairs={{0,2},{2,4},{4,6},{6,8},{8,10},{10,12},{12,14},{14,16},{16,18},{18... | collective-permute-start | bytes 786440 | tf_op jit(solution)/shard_map/ppermute | solution.py:183
  6.4 1.3 %collective-permute-start = (bf16[256,512]{1,0:T(8,128)(2,1)S(1)}, bf16[256,512]{1,0:T(8,128)(2,1)S(1)}, u32[]{:S(2)}, u32[]{:S(2)}) collective-permute-start(bf16[256,512]{1,0:T(8,128)(2,1)S(1)} %pad_maximum_fusion.4), channel_id=1, source_target_pairs={{0,1},{1,0},{2,3},{3,2},{4,5},{5,4},{6,7},{7,6},{8,9},{9,8},{10,11... | collective-permute-start | bytes 786440 | tf_op jit(solution)/shard_map/ppermute | solution.py:187
  7.7 0.7 copy.11
  8.5 0.1 reduce-window.8
  8.5 0.1 reduce
  8.6 0.1 select_reduce_fusion
  8.7 0.1 slice.45
  8.8 0.4 collective-permute-done.3.refs_3_
  9.3 5.7 %collective-permute-start.4 = (bf16[256,512]{1,0:T(8,128)(2,1)S(1)}, bf16[256,512]{1,0:T(8,128)(2,1)S(1)}, u32[]{:S(2)}, u32[]{:S(2)}) collective-permute-start(bf16[256,512]{1,0:T(8,128)(2,1)S(1)} %collective-permute-done.3.refs_3_), channel_id=1, source_target_pairs={{0,2},{2,4},{4,6},{6,8},{8,10},{10,12},{12,14},{14,16},{16,18},{18... | collective-permute-start | bytes 786440 | tf_op jit(solution)/shard_map/ppermute | solution.py:183
  15.0 0.1 pad_add_fusion.info_ref
  15.1 0.0 collective-permute-done.refs_3_
  15.2 4.4 %collective-permute-start.1 = (bf16[512,512]{1,0:T(8,128)(2,1)S(1)}, bf16[512,512]{1,0:T(8,128)(2,1)S(1)}, u32[]{:S(2)}, u32[]{:S(2)}) collective-permute-start(bf16[512,512]{1,0:T(8,128)(2,1)S(1)} %pad_maximum_fusion), channel_id=1, source_target_pairs={{0,2},{2,4},{4,6},{6,8},{8,10},{10,12},{12,14},{14,16},{16,18},{18... | collective-permute-start | bytes 1572872 | tf_op jit(solution)/shard_map/ppermute | solution.py:183
  19.6 0.0 collective-permute-done.2.refs_0_
  19.6 0.0 collective-permute-done.4.refs_1_
  19.6 18.5 %attention.2 = (bf16[512,4096]{1,0:T(8,128)(2,1)}, bf16[256,512]{1,0:T(8,128)(2,1)S(1)}, bf16[256,512]{1,0:T(8,128)(2,1)S(1)}, f32[256,512]{1,0:T(8,128)S(1)}, f32[256,512]{1,0:T(8,128)S(1)}) custom-call(s32[6]{0:T(128)S(1)} %pad_add_fusion.info_ref, s32[1,512]{1,0:T(1,128)S(1)} %bitcast.4, bf16[512,4096]{1,0:T(8,128)(2,1)} %q_ref.3, ...), custom_call_target="tpu_custom_call" | custom-call | flops 5368709120 | bytes 6291456 | tf_op jit(solution)/shard_map/attention/pallas_call | solution.py:144
  38.1 1.9 %collective-permute-start.5 = (bf16[512,512]{1,0:T(8,128)(2,1)S(1)}, bf16[512,512]{1,0:T(8,128)(2,1)S(1)}, u32[]{:S(2)}, u32[]{:S(2)}) collective-permute-start(bf16[512,512]{1,0:T(8,128)(2,1)S(1)} %pad_maximum_fusion.1), channel_id=1, source_target_pairs={{2,0},{4,2},{6,4},{8,6},{10,8},{12,10},{14,12},{16,14},{18,16},{20... | collective-permute-start | bytes 1572872 | tf_op jit(solution)/shard_map/ppermute | solution.py:183
  40.0 0.0 collective-permute-done.1
  40.1 18.6 %attention.3 = (bf16[512,4096]{1,0:T(8,128)(2,1)}, bf16[256,512]{1,0:T(8,128)(2,1)S(1)}, bf16[256,512]{1,0:T(8,128)(2,1)S(1)}, f32[256,512]{1,0:T(8,128)S(1)}, f32[256,512]{1,0:T(8,128)S(1)}) custom-call(s32[6]{0:T(128)S(1)} %pad_add_fusion.info_ref, s32[1,512]{1,0:T(1,128)S(1)} %bitcast.5, ...), custom_call_target="tpu_custom_call", output_to_operand_aliasing={{0}: (8, {})} | custom-call | flops 5368709120 | bytes 6291456 | tf_op jit(solution)/shard_map/attention/pallas_call | solution.py:144
  58.8 1.9 %collective-permute-start.7 = (bf16[512,512]{1,0:T(8,128)(2,1)S(1)}, bf16[512,512]{1,0:T(8,128)(2,1)S(1)}, u32[]{:S(2)}, u32[]{:S(2)}) collective-permute-start(bf16[512,512]{1,0:T(8,128)(2,1)S(1)} %pad_maximum_fusion.2), channel_id=1, source_target_pairs={{2,0},{4,2},{6,4},{8,6},{10,8},{12,10},{14,12},{16,14},{18,16},{20... | collective-permute-start | bytes 1572872 | tf_op jit(solution)/shard_map/ppermute | solution.py:183
  60.7 0.0 collective-permute-done.5
  60.7 0.2 add_convert_fusion.2
  60.9 0.3 collective-permute-start.6
  61.1 0.1 broadcast.31.clone.1
  61.2 0.1 broadcast.31.clone
  61.3 8.8 %collective-permute-done.7 = bf16[512,512]{1,0:T(8,128)(2,1)S(1)} collective-permute-done((bf16[512,512]{1,0:T(8,128)(2,1)S(1)}, bf16[512,512]{1,0:T(8,128)(2,1)S(1)}, u32[]{:S(2)}, u32[]{:S(2)}) %collective-permute-start.7) | collective-permute-done | bytes 524320 | tf_op jit(solution)/shard_map/ppermute | solution.py:183
  70.2 0.2 add_convert_fusion
  70.3 0.3 collective-permute-start.8
  70.6 0.0 collective-permute-done.6
  70.7 4.9 %collective-permute-done.8 = bf16[256,512]{1,0:T(8,128)(2,1)S(1)} collective-permute-done((bf16[256,512]{1,0:T(8,128)(2,1)S(1)}, bf16[256,512]{1,0:T(8,128)(2,1)S(1)}, u32[]{:S(2)}, u32[]{:S(2)}) %collective-permute-start.8) | collective-permute-done | bytes 262176 | tf_op jit(solution)/shard_map/ppermute | solution.py:187
  75.6 0.0 copy-start
  75.7 0.0 copy-start.1
  75.7 0.8 %copy-done = bf16[256,1024]{1,0:T(8,128)(2,1)} copy-done((bf16[256,1024]{1,0:T(8,128)(2,1)}, bf16[256,1024]{1,0:T(8,128)(2,1)S(1)}, u32[]{:S(2)}) %copy-start) | copy-done | bytes 524312
  76.4 0.2 copy-done.1
  (15 shorter events, 0.4 us)
Async XLA Ops:
  2.0 7.2 %collective-permute-start.3 = (bf16[256,512]{1,0:T(8,128)(2,1)S(1)}, bf16[256,512]{1,0:T(8,128)(2,1)S(1)}, u32[]{:S(2)}, u32[]{:S(2)}) collective-permute-start(bf16[256,512]{1,0:T(8,128)(2,1)S(1)} %pad_maximum_fusion.6), channel_id=1, source_target_pairs={{0,1},{1,0},{2,3},{3,2},{4,5},{5,4},{6,7},{7,6},{8,9},{9,8},{10,11... | collective-permute-start | bytes 786440 | tf_op jit(solution)/shard_map/ppermute | solution.py:187
  2.4 17.2 %collective-permute-start.2 = (bf16[256,512]{1,0:T(8,128)(2,1)S(1)}, bf16[256,512]{1,0:T(8,128)(2,1)S(1)}, u32[]{:S(2)}, u32[]{:S(2)}) collective-permute-start(bf16[256,512]{1,0:T(8,128)(2,1)S(1)} %pad_maximum_fusion.5.refs_2_), channel_id=1, source_target_pairs={{0,2},{2,4},{4,6},{6,8},{8,10},{10,12},{12,14},{14,16},{16,18},{18... | collective-permute-start | bytes 786440 | tf_op jit(solution)/shard_map/ppermute | solution.py:183
  6.4 8.7 %collective-permute-start = (bf16[256,512]{1,0:T(8,128)(2,1)S(1)}, bf16[256,512]{1,0:T(8,128)(2,1)S(1)}, u32[]{:S(2)}, u32[]{:S(2)}) collective-permute-start(bf16[256,512]{1,0:T(8,128)(2,1)S(1)} %pad_maximum_fusion.4), channel_id=1, source_target_pairs={{0,1},{1,0},{2,3},{3,2},{4,5},{5,4},{6,7},{7,6},{8,9},{9,8},{10,11... | collective-permute-start | bytes 786440 | tf_op jit(solution)/shard_map/ppermute | solution.py:187
  9.3 10.3 %collective-permute-start.4 = (bf16[256,512]{1,0:T(8,128)(2,1)S(1)}, bf16[256,512]{1,0:T(8,128)(2,1)S(1)}, u32[]{:S(2)}, u32[]{:S(2)}) collective-permute-start(bf16[256,512]{1,0:T(8,128)(2,1)S(1)} %collective-permute-done.3.refs_3_), channel_id=1, source_target_pairs={{0,2},{2,4},{4,6},{6,8},{8,10},{10,12},{12,14},{14,16},{16,18},{18... | collective-permute-start | bytes 786440 | tf_op jit(solution)/shard_map/ppermute | solution.py:183
  15.2 24.8 %collective-permute-start.1 = (bf16[512,512]{1,0:T(8,128)(2,1)S(1)}, bf16[512,512]{1,0:T(8,128)(2,1)S(1)}, u32[]{:S(2)}, u32[]{:S(2)}) collective-permute-start(bf16[512,512]{1,0:T(8,128)(2,1)S(1)} %pad_maximum_fusion), channel_id=1, source_target_pairs={{0,2},{2,4},{4,6},{6,8},{8,10},{10,12},{12,14},{14,16},{16,18},{18... | collective-permute-start | bytes 1572872 | tf_op jit(solution)/shard_map/ppermute | solution.py:183
  38.1 22.6 %collective-permute-start.5 = (bf16[512,512]{1,0:T(8,128)(2,1)S(1)}, bf16[512,512]{1,0:T(8,128)(2,1)S(1)}, u32[]{:S(2)}, u32[]{:S(2)}) collective-permute-start(bf16[512,512]{1,0:T(8,128)(2,1)S(1)} %pad_maximum_fusion.1), channel_id=1, source_target_pairs={{2,0},{4,2},{6,4},{8,6},{10,8},{12,10},{14,12},{16,14},{18,16},{20... | collective-permute-start | bytes 1572872 | tf_op jit(solution)/shard_map/ppermute | solution.py:183
  58.8 11.4 %collective-permute-start.7 = (bf16[512,512]{1,0:T(8,128)(2,1)S(1)}, bf16[512,512]{1,0:T(8,128)(2,1)S(1)}, u32[]{:S(2)}, u32[]{:S(2)}) collective-permute-start(bf16[512,512]{1,0:T(8,128)(2,1)S(1)} %pad_maximum_fusion.2), channel_id=1, source_target_pairs={{2,0},{4,2},{6,4},{8,6},{10,8},{12,10},{14,12},{16,14},{18,16},{20... | collective-permute-start | bytes 1572872 | tf_op jit(solution)/shard_map/ppermute | solution.py:183
  60.9 9.7 %collective-permute-start.6 = (bf16[256,512]{1,0:T(8,128)(2,1)S(1)}, bf16[256,512]{1,0:T(8,128)(2,1)S(1)}, u32[]{:S(2)}, u32[]{:S(2)}) collective-permute-start(bf16[256,512]{1,0:T(8,128)(2,1)S(1)} %get-tuple-element.25), channel_id=1, source_target_pairs={{0,1},{1,0},{2,3},{3,2},{4,5},{5,4},{6,7},{7,6},{8,9},{9,8},{10,11... | collective-permute-start | bytes 786440 | tf_op jit(solution)/shard_map/ppermute | solution.py:187
  70.3 5.3 %collective-permute-start.8 = (bf16[256,512]{1,0:T(8,128)(2,1)S(1)}, bf16[256,512]{1,0:T(8,128)(2,1)S(1)}, u32[]{:S(2)}, u32[]{:S(2)}) collective-permute-start(bf16[256,512]{1,0:T(8,128)(2,1)S(1)} %get-tuple-element.23), channel_id=1, source_target_pairs={{0,1},{1,0},{2,3},{3,2},{4,5},{5,4},{6,7},{7,6},{8,9},{9,8},{10,11... | collective-permute-start | bytes 786440 | tf_op jit(solution)/shard_map/ppermute | solution.py:187
  75.6 0.8 %copy-start = (bf16[256,1024]{1,0:T(8,128)(2,1)}, bf16[256,1024]{1,0:T(8,128)(2,1)S(1)}, u32[]{:S(2)}) copy-start(bf16[256,1024]{1,0:T(8,128)(2,1)S(1)} %get-tuple-element.37) | copy-start | bytes 1572868
  75.7 1.0 %copy-start.1 = (bf16[256,1024]{1,0:T(8,128)(2,1)}, bf16[256,1024]{1,0:T(8,128)(2,1)S(1)}, u32[]{:S(2)}) copy-start(bf16[256,1024]{1,0:T(8,128)(2,1)S(1)} %get-tuple-element.38) | copy-start | bytes 1572868
